TPU v7x, 32 devices: a whole 2x2x4 slice. The times are simulated.
32 devices in a mesh: grp: 2 (over x), blk: 16 (over z, y, core).
Axes of the slice: x: 2, y: 2, z: 4, core: 2. Of those that a mesh axis runs over, the one named last changes fastest.
Arguments:
- zonal_velocity_field: bfloat16 [512, 64, 128], P('blk'), may hold values from -6 to 6
- meridional_velocity_field: bfloat16 [512, 64, 128], P('blk'), may hold values from -6 to 6
- barometric_disturbance: bfloat16 [512, 64, 128], P('blk'), may hold values from -6 to 6
- delayed_thermal_deviation: bfloat16 [512, 64, 128], P('blk'), may hold values from -6 to 6
- delayed_moisture_deviation: bfloat16 [512, 64, 128], P('blk'), may hold values from -6 to 6
- flow_category_label: int32 [512, 64], P('blk'), may hold values from 0 to 15, as said below
- advective_stability_number: float32 [128], replicated, may hold values from 0.25 to 1.3
- initial_dense_matrix: bfloat16 [16, 256, 1024], P('blk'), may hold values from -0.5 to 0.5
- middle_dense_matrix: bfloat16 [16, 1024, 1024], P('blk'), may hold values from -0.25 to 0.25
- closing_dense_matrix: bfloat16 [16, 1024, 1024], P('blk'), may hold values from -0.25 to 0.25
- final_readout_matrix: bfloat16 [16, 1024, 256], P('blk'), may hold values from -0.25 to 0.25
Outputs:
- new_east: bfloat16 [512, 64, 128], P('blk', 'grp')
- new_north: bfloat16 [512, 64, 128], P('blk', 'grp')
- new_pressure: bfloat16 [512, 64, 128], P('blk', 'grp')
- heating: bfloat16 [512, 64, 128], P('blk', 'grp')
- moistening: bfloat16 [512, 64, 128], P('blk', 'grp')
Inputs may be any that keep to these rules, and one draw needn't show every extreme that they name: Each tile block, rows 32 * b to 32 * b + 31 of flow_category_label, holds exactly 128 columns of every regime.
All inputs are finite; a program needn't handle non-finite values.
Results may differ from a plain program's by a relative error of at most 0.012.
Values may be sent and summed in bfloat16 or wider, within the bound.
No kernel may reach another device: no remote copies, remote signals or barrier semaphores. Data moves between devices by JAX's collectives and lax.ppermute only.
A program may use at most 64 MiB of HBM per device.

v0:
```python
import jax
import jax.numpy as jnp
from jax import lax
from jax.sharding import PartitionSpec as P

HEIGHT_COUNT = 128
SUB = 4


def with_halo(cells, sides, width):
    for axis, dim in sides:
        count = lax.axis_size(axis)
        head = lax.slice_in_dim(cells, 0, width, axis=dim)
        tail = lax.slice_in_dim(cells, cells.shape[dim] - width, cells.shape[dim], axis=dim)
        cells = jnp.concatenate(
            [
                lax.ppermute(tail, axis, [(i, (i + 1) % count) for i in range(count)]),
                cells,
                lax.ppermute(head, axis, [((i + 1) % count, i) for i in range(count)]),
            ],
            axis=dim,
        )
    return cells


def cycle_diff(field):
    return (field[2:] - field[:-2]) * 0.5


def across_belt(field):
    padded = jnp.pad(field, ((0, 0), (1, 1), (0, 0)))
    return (padded[:, 2:] - padded[:, :-2]) * 0.5


def margin(field):
    return jnp.pad(field, ((1, 1), (0, 0), (0, 0)))


def faces(field):
    return with_halo(field.astype(jnp.bfloat16), (("blk", 0),), 1).astype(field.dtype)


def wind_update(eastward, northward, pressure_state, courant_rate):
    inner = pressure_state[1:-1]
    return (
        eastward[1:-1] - courant_rate * cycle_diff(pressure_state),
        northward[1:-1] - courant_rate * across_belt(inner),
        inner,
    )


def pressure_update(eastward, northward, pressure_state, courant_rate):
    inner_north = northward[1:-1]
    return (
        eastward[1:-1],
        inner_north,
        pressure_state[1:-1] - courant_rate * (cycle_diff(eastward) + across_belt(inner_north)),
    )


def network(columns, first, second, third, last):
    hidden = jax.nn.silu(jnp.dot(columns, first, preferred_element_type=jnp.float32)).astype(
        jnp.bfloat16
    )
    hidden = jax.nn.silu(jnp.dot(hidden, second, preferred_element_type=jnp.float32)).astype(
        jnp.bfloat16
    )
    hidden = jax.nn.silu(jnp.dot(hidden, third, preferred_element_type=jnp.float32)).astype(
        jnp.bfloat16
    )
    return jnp.dot(hidden, last, preferred_element_type=jnp.float32).astype(jnp.bfloat16)


def local(
    zonal_velocity_field,
    meridional_velocity_field,
    barometric_disturbance,
    delayed_thermal_deviation,
    delayed_moisture_deviation,
    flow_category_label,
    advective_stability_number,
    initial_dense_matrix,
    middle_dense_matrix,
    closing_dense_matrix,
    final_readout_matrix,
):
    group_index = lax.axis_index("grp")
    column_profile_width = 2 * HEIGHT_COUNT
    blocks = lax.axis_size("blk")
    atmosphere_soundings = jnp.concatenate(
        [delayed_thermal_deviation, delayed_moisture_deviation], axis=-1
    ).reshape(-1, column_profile_width)
    share = atmosphere_soundings.shape[0] // blocks
    sorting = jnp.argsort(flow_category_label.reshape(-1), stable=True)
    outgoing = jnp.take(atmosphere_soundings, sorting, axis=0).reshape(
        blocks, share, column_profile_width
    )
    half_width = zonal_velocity_field.shape[1] // 2
    pair_size = lax.axis_size("grp")
    part_rows = share // pair_size
    chosen = lax.dynamic_slice_in_dim(outgoing, group_index * part_rows, part_rows, 1)
    chosen_places = lax.dynamic_slice_in_dim(
        sorting.reshape(blocks, share), group_index * part_rows, part_rows, 1
    )
    arrived = lax.all_to_all(chosen, "blk", split_axis=0, concat_axis=0, tiled=True)
    columns = arrived.reshape(-1, column_profile_width)
    result = network(
        columns,
        initial_dense_matrix[0],
        middle_dense_matrix[0],
        closing_dense_matrix[0],
        final_readout_matrix[0],
    ).reshape(arrived.shape)
    returned = lax.all_to_all(result, "blk", split_axis=0, concat_axis=0, tiled=True)
    restored = (
        jnp.zeros((atmosphere_soundings.shape[0], column_profile_width), jnp.float32)
        .at[chosen_places.reshape(-1)]
        .set(returned.reshape(-1, column_profile_width).astype(jnp.float32))
    )
    tendency = restored.reshape(
        zonal_velocity_field.shape[0], zonal_velocity_field.shape[1], column_profile_width
    )
    heat_half, moist_half = (
        lax.psum_scatter(
            tendency[:, :, :HEIGHT_COUNT].astype(jnp.bfloat16),
            "grp",
            scatter_dimension=1,
            tiled=True,
        ).astype(jnp.float32),
        lax.psum_scatter(
            tendency[:, :, HEIGHT_COUNT:].astype(jnp.bfloat16),
            "grp",
            scatter_dimension=1,
            tiled=True,
        ).astype(jnp.float32),
    )
    eastward = zonal_velocity_field.astype(jnp.float32)
    northward = meridional_velocity_field.astype(jnp.float32)
    pressure_state = barometric_disturbance.astype(jnp.float32)
    for substep in range(SUB):
        eastward, northward, pressure_state = wind_update(
            margin(eastward), margin(northward), faces(pressure_state), advective_stability_number
        )
        eastward, northward, pressure_state = pressure_update(
            faces(eastward), margin(northward), margin(pressure_state), advective_stability_number
        )
    dynamic_fields = (
        eastward.astype(jnp.bfloat16),
        northward.astype(jnp.bfloat16),
        pressure_state.astype(jnp.bfloat16),
    )
    own_start = group_index * half_width
    owned = [lax.dynamic_slice_in_dim(field, own_start, half_width, 1) for field in dynamic_fields]
    return (
        owned[0],
        owned[1],
        owned[2],
        heat_half.astype(jnp.bfloat16),
        moist_half.astype(jnp.bfloat16),
    )


def solution(mesh):
    return jax.shard_map(
        local,
        mesh=mesh,
        in_specs=(
            P("blk", None, None),
            P("blk", None, None),
            P("blk", None, None),
            P("blk", None, None),
            P("blk", None, None),
            P("blk", None),
            P(),
            P("blk", None, None),
            P("blk", None, None),
            P("blk", None, None),
            P("blk", None, None),
        ),
        out_specs=(
            P("blk", "grp", None),
            P("blk", "grp", None),
            P("blk", "grp", None),
            P("blk", "grp", None),
            P("blk", "grp", None),
        ),
        check_vma=False,
    )
```

profile of v0, /device:TPU:0, one launch (start us, length us, event | category | flops | bytes accessed | tf_op | source)
XLA Modules:
  0.0 156.3 jit_solution(10562687520552470233)
XLA Ops:
  7.2 0.9 fusion.74
  8.1 5.4 %collective-permute-start.1 = (bf16[1,64,128]{2,1,0:T(8,128)(2,1)S(1)}, bf16[1,64,128]{2,1,0:T(8,128)(2,1)S(1)}, u32[]{:S(2)}, u32[]{:S(2)}) collective-permute-start(bf16[1,64,128]{2,1,0:T(8,128)(2,1)S(1)} %get-tuple-element.36), channel_id=1, source_target_pairs={{1,0},{2,1},{3,2},{4,3},{5,4},{6,5},{7,6},{8,7},{9,8},{10,9},{11,1... | collective-permute-start | bytes 49160 | tf_op jit(solution)/shard_map/ppermute | solution.py:19
  13.5 0.8 reshape.75
  14.3 5.0 %sort.17 = (s32[2048]{0:T(1024)}, s32[2048]{0:T(1024)S(1)}) sort(s32[2048]{0:T(1024)S(1)} %reshape.75, s32[2048]{0:T(1024)S(1)} %iota.4), dimensions={0}, to_apply=%region_0.0 | sort | flops 22528 | bytes 32768 | tf_op jit(solution)/shard_map/jit(argsort)/sort | solution.py:94
  19.4 1.3 pad_maximum_fusion
  20.7 9.0 %gather_fusion = bf16[2048,256]{1,0:T(8,128)(2,1)} fusion(bf16[2048,256]{1,0:T(8,128)(2,1)S(1)} %bitcast.29, s32[2048]{0:T(1024)S(1)} %fusion.60), kind=kCustom, calls=%fused_computation | custom fusion | bytes 2105344 | tf_op jit(solution)/shard_map/jit(_take)/gather | solution.py:95
  29.8 2.1 %dynamic-slice_select_fusion = bf16[16,64,256]{2,1,0:T(8,128)(2,1)} fusion(bf16[16,128,256]{2,1,0:T(8,128)(2,1)} %bitcast.31, s32[]{:T(128)S(6)} %select_n.30, pred[16,64]{1,0:T(8,128)(4,1)S(1)} %constant_dynamic-slice_fusion), kind=kLoop, calls=%fused_computation.86 | loop fusion | flops 262144 | bytes 1049604 | tf_op jit(solution)/shard_map/jit(_take)/select_n | solution.py:95
  32.0 5.9 %all-to-all-start = ((bf16[16,64,256]{2,1,0:T(8,128)(2,1)}), bf16[16,64,256]{2,1,0:T(8,128)(2,1)}, u32[]{:S(2)}, u32[]{:S(2)}) async-start(bf16[16,64,256]{2,1,0:T(8,128)(2,1)} %dynamic-slice_select_fusion), calls=%async_computation | async-start | bytes 1048576 | tf_op jit(solution)/shard_map/all_to_all | solution.py:105
  38.3 4.4 %collective-permute-start.3 = (bf16[1,64,128]{2,1,0:T(8,128)(2,1)S(1)}, bf16[1,64,128]{2,1,0:T(8,128)(2,1)S(1)}, u32[]{:S(2)}, u32[]{:S(2)}) collective-permute-start(bf16[1,64,128]{2,1,0:T(8,128)(2,1)S(1)} %get-tuple-element.34), channel_id=1, source_target_pairs={{1,0},{2,1},{3,2},{4,3},{5,4},{6,5},{7,6},{8,7},{9,8},{10,9},{11,1... | collective-permute-start | bytes 49160 | tf_op jit(solution)/shard_map/ppermute | solution.py:19
  43.0 4.5 %collective-permute-done.3 = bf16[1,64,128]{2,1,0:T(8,128)(2,1)S(1)} collective-permute-done((bf16[1,64,128]{2,1,0:T(8,128)(2,1)S(1)}, bf16[1,64,128]{2,1,0:T(8,128)(2,1)S(1)}, u32[]{:S(2)}, u32[]{:S(2)}) %collective-permute-start.3) | collective-permute-done | bytes 16416 | tf_op jit(solution)/shard_map/ppermute | solution.py:19
  47.5 4.6 %collective-permute-done.2 = bf16[1,64,128]{2,1,0:T(8,128)(2,1)S(1)} collective-permute-done((bf16[1,64,128]{2,1,0:T(8,128)(2,1)S(1)}, bf16[1,64,128]{2,1,0:T(8,128)(2,1)S(1)}, u32[]{:S(2)}, u32[]{:S(2)}) %collective-permute-start.2) | collective-permute-done | bytes 16416 | tf_op jit(solution)/shard_map/ppermute | solution.py:17
  52.2 0.4 fusion.19
  52.7 0.8 copy-done.14
  53.5 0.5 collective-permute-start.4
  54.2 0.8 collective-permute-done.5
  55.0 4.4 %collective-permute-done.4 = bf16[1,64,128]{2,1,0:T(8,128)(2,1)S(1)} collective-permute-done((bf16[1,64,128]{2,1,0:T(8,128)(2,1)S(1)}, bf16[1,64,128]{2,1,0:T(8,128)(2,1)S(1)}, u32[]{:S(2)}, u32[]{:S(2)}) %collective-permute-start.4) | collective-permute-done | bytes 16416 | tf_op jit(solution)/shard_map/ppermute | solution.py:17
  59.4 1.1 maximum_convert_fusion.2
  60.9 0.5 collective-permute-start.6
  62.3 4.5 %collective-permute-done.6 = bf16[1,64,128]{2,1,0:T(8,128)(2,1)S(1)} collective-permute-done((bf16[1,64,128]{2,1,0:T(8,128)(2,1)S(1)}, bf16[1,64,128]{2,1,0:T(8,128)(2,1)S(1)}, u32[]{:S(2)}, u32[]{:S(2)}) %collective-permute-start.6) | collective-permute-done | bytes 16416 | tf_op jit(solution)/shard_map/ppermute | solution.py:17
  66.9 0.4 fusion.27
  67.4 0.6 copy-done.3
  67.9 0.5 collective-permute-start.8
  68.4 0.9 collective-permute-done.9
  69.4 4.4 %collective-permute-done.8 = bf16[1,64,128]{2,1,0:T(8,128)(2,1)S(1)} collective-permute-done((bf16[1,64,128]{2,1,0:T(8,128)(2,1)S(1)}, bf16[1,64,128]{2,1,0:T(8,128)(2,1)S(1)}, u32[]{:S(2)}, u32[]{:S(2)}) %collective-permute-start.8) | collective-permute-done | bytes 16416 | tf_op jit(solution)/shard_map/ppermute | solution.py:17
  73.9 6.4 %fusion.2 = f32[1024,1024]{1,0:T(8,128)} fusion(bf16[1,1024,1024]{2,1,0:T(8,128)(2,1)S(1)} %copy-done, bf16[1024,256]{1,0:T(8,128)(2,1)} %bitcast.5, bf16[1,256,1024]{2,1,0:T(8,128)(2,1)} %param.18), kind=kOutput, calls=%fused_computation.7 | convolution fusion | flops 2689597440 | bytes 7340032 | tf_op jit(solution)/shard_map/dot_general | solution.py:65
  80.3 7.3 %fusion.7 = bf16[1024,256]{1,0:T(8,128)(2,1)} fusion(bf16[1,1024,1024]{2,1,0:T(8,128)(2,1)} %param.20, f32[1024,1024]{1,0:T(8,128)} %fusion.2, bf16[1,1024,256]{2,1,0:T(8,128)(2,1)} %param.21), kind=kOutput, calls=%fused_computation.11 | convolution fusion | flops 2695102464 | bytes 7340032 | tf_op jit(solution)/shard_map/dot_general | solution.py:71
  87.7 4.2 %all-to-all-start.1 = ((bf16[16,64,256]{2,1,0:T(8,128)(2,1)}), bf16[16,64,256]{2,1,0:T(8,128)(2,1)}, u32[]{:S(2)}, u32[]{:S(2)}) async-start(bf16[16,64,256]{2,1,0:T(8,128)(2,1)} %bitcast.32), calls=%async_computation.1 | async-start | bytes 1048576 | tf_op jit(solution)/shard_map/all_to_all | solution.py:114
  92.0 1.5 fusion.44
  93.6 4.3 %collective-permute-start.11 = (bf16[1,64,128]{2,1,0:T(8,128)(2,1)S(1)}, bf16[1,64,128]{2,1,0:T(8,128)(2,1)S(1)}, u32[]{:S(2)}, u32[]{:S(2)}) collective-permute-start(bf16[1,64,128]{2,1,0:T(8,128)(2,1)S(1)} %get-tuple-element.26), channel_id=1, source_target_pairs={{1,0},{2,1},{3,2},{4,3},{5,4},{6,5},{7,6},{8,7},{9,8},{10,9},{11,1... | collective-permute-start | bytes 49160 | tf_op jit(solution)/shard_map/ppermute | solution.py:19
  98.2 3.3 %collective-permute-done.11 = bf16[1,64,128]{2,1,0:T(8,128)(2,1)S(1)} collective-permute-done((bf16[1,64,128]{2,1,0:T(8,128)(2,1)S(1)}, bf16[1,64,128]{2,1,0:T(8,128)(2,1)S(1)}, u32[]{:S(2)}, u32[]{:S(2)}) %collective-permute-start.11) | collective-permute-done | bytes 16416 | tf_op jit(solution)/shard_map/ppermute | solution.py:19
  101.5 4.7 %collective-permute-done.10 = bf16[1,64,128]{2,1,0:T(8,128)(2,1)S(1)} collective-permute-done((bf16[1,64,128]{2,1,0:T(8,128)(2,1)S(1)}, bf16[1,64,128]{2,1,0:T(8,128)(2,1)S(1)}, u32[]{:S(2)}, u32[]{:S(2)}) %collective-permute-start.10) | collective-permute-done | bytes 16416 | tf_op jit(solution)/shard_map/ppermute | solution.py:17
  106.3 1.0 copy-done.1
  107.3 1.2 fusion.35
  108.5 6.7 %scatter_custom_fusion = f32[2048,256]{1,0:T(8,128)} fusion(s32[1024]{0:T(1024)S(1)} %bitcast.34, bf16[1024,256]{1,0:T(8,128)(2,1)} %bitcast.13, f32[]{:T(128)} %constant.13.clone.1), kind=kCustom, calls=%fused_computation.75 | custom fusion | flops 262144 | bytes 2621444 | tf_op jit(solution)/shard_map/scatter | solution.py:118
  115.2 1.7 %convert.7 = bf16[2048,256]{1,0:T(8,128)(2,1)S(1)} convert(f32[2048,256]{1,0:T(8,128)} %scatter_custom_fusion) | non-fusion elementwise | flops 524288 | bytes 3145728 | tf_op jit(solution)/shard_map/convert.2
  116.9 1.3 fusion.66
  118.3 0.7 fusion.68
  119.0 0.6 collective-permute-start.13
  119.6 1.4 collective-permute-done.13
  121.1 4.4 %collective-permute-done.12 = bf16[1,64,128]{2,1,0:T(8,128)(2,1)S(1)} collective-permute-done((bf16[1,64,128]{2,1,0:T(8,128)(2,1)S(1)}, bf16[1,64,128]{2,1,0:T(8,128)(2,1)S(1)}, u32[]{:S(2)}, u32[]{:S(2)}) %collective-permute-start.12) | collective-permute-done | bytes 16416 | tf_op jit(solution)/shard_map/ppermute | solution.py:17
  125.5 1.1 maximum_convert_fusion.6
  127.1 0.5 collective-permute-start.14
  128.2 1.7 %constant_dynamic-slice_fusion.2 = bf16[32,32,128]{2,1,0:T(8,128)(2,1)} fusion(bf16[32,64,128]{2,1,0:T(8,128)(2,1)} %copy-done.12, s32[]{:T(128)S(6)} %select_n.29), kind=kLoop, calls=%fused_computation.102 | loop fusion | bytes 524292 | tf_op jit(solution)/shard_map/dynamic_slice | solution.py:153
  130.2 0.8 dynamic-slice_convert_fusion
  130.9 2.0 %collective-permute-done.14 = bf16[1,64,128]{2,1,0:T(8,128)(2,1)S(1)} collective-permute-done((bf16[1,64,128]{2,1,0:T(8,128)(2,1)S(1)}, bf16[1,64,128]{2,1,0:T(8,128)(2,1)S(1)}, u32[]{:S(2)}, u32[]{:S(2)}) %collective-permute-start.14) | collective-permute-done | bytes 16416 | tf_op jit(solution)/shard_map/ppermute | solution.py:17
  133.3 1.0 copy-done.11
  134.3 1.0 fusion.54
  135.3 14.1 %reduce-scatter.5.cloned.1.call-done = bf16[32,32,128]{2,1,0:T(8,128)(2,1)} async-done(((bf16[32,64,128]{2,1,0:T(8,128)(2,1)}), bf16[32,32,128]{2,1,0:T(8,128)(2,1)}) %reduce-scatter.5.cloned.1.call-update) | async-done | bytes 262160 | tf_op jit(solution)/shard_map/reduce_scatter | solution.py:130
  (82 shorter events, 4.6 us)
Async XLA Ops:
  7.2 66.7 %copy-start = (bf16[1,1024,1024]{2,1,0:T(8,128)(2,1)S(1)}, bf16[1,1024,1024]{2,1,0:T(8,128)(2,1)}, u32[]{:S(2)}) copy-start(bf16[1,1024,1024]{2,1,0:T(8,128)(2,1)} %param.19) | copy-start | bytes 6291460
  8.1 29.8 %collective-permute-start.1 = (bf16[1,64,128]{2,1,0:T(8,128)(2,1)S(1)}, bf16[1,64,128]{2,1,0:T(8,128)(2,1)S(1)}, u32[]{:S(2)}, u32[]{:S(2)}) collective-permute-start(bf16[1,64,128]{2,1,0:T(8,128)(2,1)S(1)} %get-tuple-element.36), channel_id=1, source_target_pairs={{1,0},{2,1},{3,2},{4,3},{5,4},{6,5},{7,6},{8,7},{9,8},{10,9},{11,1... | collective-permute-start | bytes 49160 | tf_op jit(solution)/shard_map/ppermute | solution.py:19
  13.5 24.4 %collective-permute-start = (bf16[1,64,128]{2,1,0:T(8,128)(2,1)S(1)}, bf16[1,64,128]{2,1,0:T(8,128)(2,1)S(1)}, u32[]{:S(2)}, u32[]{:S(2)}) collective-permute-start(bf16[1,64,128]{2,1,0:T(8,128)(2,1)S(1)} %get-tuple-element.35), channel_id=1, source_target_pairs={{0,1},{1,2},{2,3},{3,4},{4,5},{5,6},{6,7},{7,8},{8,9},{9,10},{10,1... | collective-permute-start | bytes 49160 | tf_op jit(solution)/shard_map/ppermute | solution.py:17
  29.8 8.1 %copy-start.18 = (f32[128]{0:T(128)S(1)}, f32[128]{0:T(128)}, u32[]{:S(2)}) copy-start(f32[128]{0:T(128)} %param.17) | copy-start | bytes 1540
  29.8 8.1 %copy-start.15 = (bf16[32,64,128]{2,1,0:T(8,128)(2,1)S(1)}, bf16[32,64,128]{2,1,0:T(8,128)(2,1)}, u32[]{:S(2)}) copy-start(bf16[32,64,128]{2,1,0:T(8,128)(2,1)} %param.13) | copy-start | bytes 1572868
  29.8 8.2 %copy-start.17 = (bf16[32,64,128]{2,1,0:T(8,128)(2,1)S(1)}, bf16[32,64,128]{2,1,0:T(8,128)(2,1)}, u32[]{:S(2)}) copy-start(bf16[32,64,128]{2,1,0:T(8,128)(2,1)} %param.11) | copy-start | bytes 1572868
  32.0 41.9 %all-to-all-start = ((bf16[16,64,256]{2,1,0:T(8,128)(2,1)}), bf16[16,64,256]{2,1,0:T(8,128)(2,1)}, u32[]{:S(2)}, u32[]{:S(2)}) async-start(bf16[16,64,256]{2,1,0:T(8,128)(2,1)} %dynamic-slice_select_fusion), calls=%async_computation | async-start | bytes 1048576 | tf_op jit(solution)/shard_map/all_to_all | solution.py:105
  38.0 4.7 %copy-start.16 = (bf16[32,64,128]{2,1,0:T(8,128)(2,1)S(1)}, bf16[32,64,128]{2,1,0:T(8,128)(2,1)}, u32[]{:S(2)}) copy-start(bf16[32,64,128]{2,1,0:T(8,128)(2,1)} %param.12) | copy-start | bytes 1572868
  38.3 9.2 %collective-permute-start.3 = (bf16[1,64,128]{2,1,0:T(8,128)(2,1)S(1)}, bf16[1,64,128]{2,1,0:T(8,128)(2,1)S(1)}, u32[]{:S(2)}, u32[]{:S(2)}) collective-permute-start(bf16[1,64,128]{2,1,0:T(8,128)(2,1)S(1)} %get-tuple-element.34), channel_id=1, source_target_pairs={{1,0},{2,1},{3,2},{4,3},{5,4},{6,5},{7,6},{8,7},{9,8},{10,9},{11,1... | collective-permute-start | bytes 49160 | tf_op jit(solution)/shard_map/ppermute | solution.py:19
  42.7 9.4 %collective-permute-start.2 = (bf16[1,64,128]{2,1,0:T(8,128)(2,1)S(1)}, bf16[1,64,128]{2,1,0:T(8,128)(2,1)S(1)}, u32[]{:S(2)}, u32[]{:S(2)}) collective-permute-start(bf16[1,64,128]{2,1,0:T(8,128)(2,1)S(1)} %get-tuple-element.33), channel_id=1, source_target_pairs={{0,1},{1,2},{2,3},{3,4},{4,5},{5,6},{6,7},{7,8},{8,9},{9,10},{10,1... | collective-permute-start | bytes 49160 | tf_op jit(solution)/shard_map/ppermute | solution.py:17
  43.0 9.7 %copy-start.8 = (f32[32,64,128]{2,1,0:T(8,128)}, f32[32,64,128]{2,1,0:T(8,128)S(1)}, u32[]{:S(2)}) copy-start(f32[32,64,128]{2,1,0:T(8,128)S(1)} %fusion.14) | copy-start | bytes 3145732
  52.7 0.8 copy-start.14
  53.5 1.5 collective-permute-start.5
  53.5 5.9 %collective-permute-start.4 = (bf16[1,64,128]{2,1,0:T(8,128)(2,1)S(1)}, bf16[1,64,128]{2,1,0:T(8,128)(2,1)S(1)}, u32[]{:S(2)}, u32[]{:S(2)}) collective-permute-start(bf16[1,64,128]{2,1,0:T(8,128)(2,1)S(1)} %get-tuple-element.31), channel_id=1, source_target_pairs={{0,1},{1,2},{2,3},{3,4},{4,5},{5,6},{6,7},{7,8},{8,9},{9,10},{10,1... | collective-permute-start | bytes 49160 | tf_op jit(solution)/shard_map/ppermute | solution.py:17
  60.5 1.2 copy-start.9
  60.8 1.5 collective-permute-start.7
  60.9 5.9 %collective-permute-start.6 = (bf16[1,64,128]{2,1,0:T(8,128)(2,1)S(1)}, bf16[1,64,128]{2,1,0:T(8,128)(2,1)S(1)}, u32[]{:S(2)}, u32[]{:S(2)}) collective-permute-start(bf16[1,64,128]{2,1,0:T(8,128)(2,1)S(1)} %get-tuple-element.29), channel_id=1, source_target_pairs={{0,1},{1,2},{2,3},{3,4},{4,5},{5,6},{6,7},{7,8},{8,9},{9,10},{10,1... | collective-permute-start | bytes 49160 | tf_op jit(solution)/shard_map/ppermute | solution.py:17
  62.0 5.3 %copy-start.6 = (f32[32,64,128]{2,1,0:T(8,128)}, f32[32,64,128]{2,1,0:T(8,128)S(1)}, u32[]{:S(2)}) copy-start(f32[32,64,128]{2,1,0:T(8,128)S(1)} %fusion.22) | copy-start | bytes 3145732
  66.9 1.0 copy-start.3
  67.9 1.4 collective-permute-start.9
  67.9 5.9 %collective-permute-start.8 = (bf16[1,64,128]{2,1,0:T(8,128)(2,1)S(1)}, bf16[1,64,128]{2,1,0:T(8,128)(2,1)S(1)}, u32[]{:S(2)}, u32[]{:S(2)}) collective-permute-start(bf16[1,64,128]{2,1,0:T(8,128)(2,1)S(1)} %get-tuple-element.27), channel_id=1, source_target_pairs={{0,1},{1,2},{2,3},{3,4},{4,5},{5,6},{6,7},{7,8},{8,9},{9,10},{10,1... | collective-permute-start | bytes 49160 | tf_op jit(solution)/shard_map/ppermute | solution.py:17
  87.7 20.8 %all-to-all-start.1 = ((bf16[16,64,256]{2,1,0:T(8,128)(2,1)}), bf16[16,64,256]{2,1,0:T(8,128)(2,1)}, u32[]{:S(2)}, u32[]{:S(2)}) async-start(bf16[16,64,256]{2,1,0:T(8,128)(2,1)} %bitcast.32), calls=%async_computation.1 | async-start | bytes 1048576 | tf_op jit(solution)/shard_map/all_to_all | solution.py:114
  91.9 43.4 %reduce-scatter.3.cloned.1.call-start = ((), (), s32[]{:S(2)}) async-start(), calls=%async_computation.4 | async-start | bytes 786432 | tf_op jit(solution)/shard_map/reduce_scatter | solution.py:124
  92.0 5.9 %copy-start.7 = (f32[32,64,128]{2,1,0:T(8,128)S(1)}, f32[32,64,128]{2,1,0:T(8,128)}, u32[]{:S(2)}) copy-start(f32[32,64,128]{2,1,0:T(8,128)} %copy-done.6) | copy-start | bytes 3145732
  93.6 7.9 %collective-permute-start.11 = (bf16[1,64,128]{2,1,0:T(8,128)(2,1)S(1)}, bf16[1,64,128]{2,1,0:T(8,128)(2,1)S(1)}, u32[]{:S(2)}, u32[]{:S(2)}) collective-permute-start(bf16[1,64,128]{2,1,0:T(8,128)(2,1)S(1)} %get-tuple-element.26), channel_id=1, source_target_pairs={{1,0},{2,1},{3,2},{4,3},{5,4},{6,5},{7,6},{8,7},{9,8},{10,9},{11,1... | collective-permute-start | bytes 49160 | tf_op jit(solution)/shard_map/ppermute | solution.py:19
  97.9 8.3 %collective-permute-start.10 = (bf16[1,64,128]{2,1,0:T(8,128)(2,1)S(1)}, bf16[1,64,128]{2,1,0:T(8,128)(2,1)S(1)}, u32[]{:S(2)}, u32[]{:S(2)}) collective-permute-start(bf16[1,64,128]{2,1,0:T(8,128)(2,1)S(1)} %get-tuple-element.25), channel_id=1, source_target_pairs={{0,1},{1,2},{2,3},{3,4},{4,5},{5,6},{6,7},{7,8},{8,9},{9,10},{10,1... | collective-permute-start | bytes 49160 | tf_op jit(solution)/shard_map/ppermute | solution.py:17
  98.2 8.1 %copy-start.4 = (f32[32,64,128]{2,1,0:T(8,128)}, f32[32,64,128]{2,1,0:T(8,128)S(1)}, u32[]{:S(2)}) copy-start(f32[32,64,128]{2,1,0:T(8,128)S(1)} %fusion.30) | copy-start | bytes 3145732
  106.3 1.0 copy-start.1
  116.9 9.7 %copy-start.2 = (f32[34,64,128]{2,1,0:T(8,128)S(1)}, f32[34,64,128]{2,1,0:T(8,128)}, u32[]{:S(2)}) copy-start(f32[34,64,128]{2,1,0:T(8,128)} %copy-done.1) | copy-start | bytes 3342340
  118.2 31.2 %reduce-scatter.5.cloned.1.call-start = ((), (), s32[]{:S(2)}) async-start(), calls=%async_computation.5 | async-start | bytes 786432 | tf_op jit(solution)/shard_map/reduce_scatter | solution.py:130
  119.0 2.0 %collective-permute-start.13 = (bf16[1,64,128]{2,1,0:T(8,128)(2,1)S(1)}, bf16[1,64,128]{2,1,0:T(8,128)(2,1)S(1)}, u32[]{:S(2)}, u32[]{:S(2)}) collective-permute-start(bf16[1,64,128]{2,1,0:T(8,128)(2,1)S(1)} %get-tuple-element.24), channel_id=1, source_target_pairs={{1,0},{2,1},{3,2},{4,3},{5,4},{6,5},{7,6},{8,7},{9,8},{10,9},{11,1... | collective-permute-start | bytes 49160 | tf_op jit(solution)/shard_map/ppermute | solution.py:19
  119.6 5.9 %collective-permute-start.12 = (bf16[1,64,128]{2,1,0:T(8,128)(2,1)S(1)}, bf16[1,64,128]{2,1,0:T(8,128)(2,1)S(1)}, u32[]{:S(2)}, u32[]{:S(2)}) collective-permute-start(bf16[1,64,128]{2,1,0:T(8,128)(2,1)S(1)} %get-tuple-element.23), channel_id=1, source_target_pairs={{0,1},{1,2},{2,3},{3,4},{4,5},{5,6},{6,7},{7,8},{8,9},{9,10},{10,1... | collective-permute-start | bytes 49160 | tf_op jit(solution)/shard_map/ppermute | solution.py:17
  126.6 1.2 copy-start.5
  127.0 1.1 copy-start.10
  127.0 1.1 copy-start.12
  127.0 3.9 %collective-permute-start.15 = (bf16[1,64,128]{2,1,0:T(8,128)(2,1)S(1)}, bf16[1,64,128]{2,1,0:T(8,128)(2,1)S(1)}, u32[]{:S(2)}, u32[]{:S(2)}) collective-permute-start(bf16[1,64,128]{2,1,0:T(8,128)(2,1)S(1)} %get-tuple-element.22), channel_id=1, source_target_pairs={{1,0},{2,1},{3,2},{4,3},{5,4},{6,5},{7,6},{8,7},{9,8},{10,9},{11,1... | collective-permute-start | bytes 49160 | tf_op jit(solution)/shard_map/ppermute | solution.py:19
  127.1 5.9 %collective-permute-start.14 = (bf16[1,64,128]{2,1,0:T(8,128)(2,1)S(1)}, bf16[1,64,128]{2,1,0:T(8,128)(2,1)S(1)}, u32[]{:S(2)}, u32[]{:S(2)}) collective-permute-start(bf16[1,64,128]{2,1,0:T(8,128)(2,1)S(1)} %get-tuple-element.21), channel_id=1, source_target_pairs={{0,1},{1,2},{2,3},{3,4},{4,5},{5,6},{6,7},{7,8},{8,9},{9,10},{10,1... | collective-permute-start | bytes 49160 | tf_op jit(solution)/shard_map/ppermute | solution.py:17
  128.1 4.8 %copy-start.13 = (bf16[32,64,128]{2,1,0:T(8,128)(2,1)S(1)}, bf16[32,64,128]{2,1,0:T(8,128)(2,1)}, u32[]{:S(2)}) copy-start(bf16[32,64,128]{2,1,0:T(8,128)(2,1)} %copy-done.12) | copy-start | bytes 1572868
  133.1 1.2 copy-start.11
Sparse Core Ops, SparseCore 0:
  118.3 13.5 reduce-scatter.2
  134.9 14.5 reduce-scatter.4
where the time goes:
time: 157 us; the launch traced here: 156 us
  waiting for transfers between devices  54.5 us (35%)
  starting transfers between devices  27.1 us (17%)
  other arithmetic  26.3 us (17%)
  local copies, waits for them, and re-layouts  20 us (13%)
  between operations  14.5 us (9%)
  matrix products  13.8 us (9%)
    ppermute x8, waiting for transfers between devices, with_halo(): lax.ppermute(tail, axis, [(i, (i + 1) % count) for i in range(count)])  29.1 us
    ppermute x8, starting transfers between devices, with_halo(): lax.ppermute(head, axis, [((i + 1) % count, i) for i in range(count)])  14.9 us
    reduce_scatter x1, waiting for transfers between devices, local(): lax.psum_scatter(tendency[:, :, HEIGHT_COUNT:].astype(jnp.bfloat16), 'grp...  14.1 us
    ppermute x8, waiting for transfers between devices, with_halo(): lax.ppermute(head, axis, [((i + 1) % count, i) for i in range(count)])  11.2 us
    gather x1, local copies, waits for them, and re-layouts, local(): jnp.take(atmosphere_soundings, sorting, axis=0)  9.03 us
    dot_general x1, matrix products, network(): jnp.dot(hidden, last, preferred_element_type=jnp.float32)  7.34 us
    scatter x1, other arithmetic, local(): restored = jnp.zeros((atmosphere_soundings.shape[0], column_profile_width...  6.69 us
    dot_general x1, matrix products, network(): jnp.dot(hidden, second, preferred_element_type=jnp.float32)  6.44 us
  transfers between devices with their start and end apart: 20, of which 14 were waited for; matrix products, arithmetic and copies ran while one was open for 20% of the time, Pallas kernels for 0%

commit v1 on v0

v1 whole, which is shorter than its diff:
```python
import functools
import jax
import jax.numpy as jnp
from jax import lax
from jax.experimental import pallas as pl
from jax.experimental.pallas import tpu as pltpu
from jax.sharding import PartitionSpec as P

SUB = 4
CHUNKS = 2
LANES = 128
MIB = 1 << 20
bf16, f32, i32 = jnp.bfloat16, jnp.float32, jnp.int32


def params(mib):
    return pltpu.CompilerParams(vmem_limit_bytes=mib * MIB)


def cost(flops, moved):
    return pl.CostEstimate(flops=flops, bytes_accessed=moved, transcendentals=0)


def folded(labels, start, half):
    rows = labels.shape[0] * half // LANES
    side = labels[:, start : start + half]
    return jnp.concatenate(
        [side[t * rows : (t + 1) * rows] for t in range(LANES // half)], axis=1
    )


def ranked(labels, regimes):
    rows = labels.shape[0]
    shape = (regimes, rows, LANES)
    member = jnp.where(
        lax.broadcasted_iota(i32, shape, 0) == jnp.broadcast_to(labels[None], shape), 1.0, 0.0
    )
    flat = member.reshape(regimes * rows, LANES).astype(bf16)
    first = lax.broadcasted_iota(i32, (LANES, LANES), 0)
    second = lax.broadcasted_iota(i32, (LANES, LANES), 1)
    earlier = jnp.where(first < second, 1.0, 0.0).astype(bf16)
    within = jnp.dot(flat, earlier, preferred_element_type=f32).reshape(shape)
    totals = jnp.dot(
        flat, jnp.ones((LANES, LANES), bf16), preferred_element_type=f32
    ).reshape(shape)
    before = jnp.zeros((regimes, 1, LANES), f32)
    rank = jnp.zeros((rows, LANES), f32)
    row_ranks = []
    for m in range(rows):
        row_ranks.append(
            jnp.sum(member[:, m : m + 1] * (within[:, m : m + 1] + before), axis=0)
        )
        before = before + totals[:, m : m + 1]
    rank = jnp.concatenate(row_ranks, axis=0)
    return rank, member, before


def route_kernel(regimes, part, group_ref, label_ref, heat_ref, moist_ref, *out_refs):
    labels = label_ref[...]
    deep, wide = labels.shape
    half = wide // 2
    rows = deep * half // LANES
    mine = group_ref[0]
    width = part // len(out_refs)
    slots = []
    for side in range(2):
        index = folded(labels, side * half, half)
        rank, _, _ = ranked(index, regimes)
        place = jnp.where(mine == side, part - 1.0 - rank, rank - part)
        slots.append((place, index.astype(f32) * width))
    columns = []
    for side in range(2):
        for m in range(rows):
            for t in range(LANES // half):
                at = (m + rows * t, slice(side * half, (side + 1) * half))
                columns.append(jnp.concatenate([heat_ref[at], moist_ref[at]], axis=1))
    soundings = jnp.concatenate(columns, axis=0)
    for k, out_ref in enumerate(out_refs):
        target = []
        for place, base in slots:
            near = place - k * width
            target.append(jnp.where((near >= 0) & (near < width), base + near, -1.0))
        total = out_ref.shape[0]
        tile = min(256, total)
        for start in range(0, total, tile):
            slot = (lax.broadcasted_iota(i32, (tile, LANES), 0) + start).astype(f32)
            picks = jnp.concatenate(
                [
                    jnp.where(slot == one[m : m + 1], 1.0, 0.0).astype(bf16)
                    for one in target
                    for m in range(rows)
                ],
                axis=1,
            )
            out_ref[start : start + tile] = jnp.dot(
                picks, soundings, preferred_element_type=f32
            ).astype(bf16)


def plan_kernel(regimes, part, chunks, group_ref, label_ref, column_ref, pack_ref):
    labels = label_ref[...]
    half = labels.shape[1] // 2
    mine = group_ref[0]
    width = part // chunks
    sides = []
    for side in range(2):
        index = folded(labels, side * half, half)
        rank, member, count = ranked(index, regimes)
        sides.append((index.astype(f32), rank, member, jnp.maximum(count - part, 0.0)))
    own = [jnp.where(mine == 0, a, b) for a, b in zip(*sides)]
    other = [jnp.where(mine == 0, b, a) for a, b in zip(*sides)]
    lane = lax.broadcasted_iota(i32, (1, LANES), 1)
    for k in range(chunks):
        index, rank, member, spare = own
        spare = jnp.clip(spare - k * width, 0.0, width)
        offset = jnp.zeros((1, LANES), f32)
        at = jnp.zeros(rank.shape, f32)
        for r in range(regimes):
            at = at + member[r] * offset
            offset = offset + spare[r]
        near = part - 1.0 - rank - k * width
        kept = jnp.where((near >= 0) & (near < width), index * width + near, -1.0)
        near = rank - part - k * width
        come = jnp.where((near >= 0) & (near < width), at + near, -1.0)
        rows = rank.shape[0]
        column_ref[:, 2 * k * rows : (2 * k + 1) * rows] = kept.T
        column_ref[:, (2 * k + 1) * rows : (2 * k + 2) * rows] = come.T
        spare = jnp.clip(other[3] - k * width, 0.0, width)
        offset = jnp.zeros((1, LANES), f32)
        per_row = LANES // width
        for r in range(regimes):
            if r % per_row == 0:
                line = jnp.full((1, LANES), -1.0)
            near = (lane - (r % per_row) * width).astype(f32)
            line = jnp.where((near >= 0) & (near < spare[r]), offset + near, line)
            offset = offset + spare[r]
            if r % per_row == per_row - 1:
                pack_ref[k, r // per_row : r // per_row + 1] = line


def pack_kernel(pack_ref, result_ref, out_ref):
    room = out_ref.shape[0]
    slot = lax.broadcasted_iota(i32, (room, LANES), 0).astype(f32)
    picks = jnp.concatenate(
        [
            jnp.where(slot == pack_ref[m : m + 1], 1.0, 0.0).astype(bf16)
            for m in range(pack_ref.shape[0])
        ],
        axis=1,
    )
    out_ref[...] = jnp.dot(picks, result_ref[...], preferred_element_type=f32).astype(bf16)


def place_kernel(chunks, column_ref, *refs):
    sources = refs[: 2 * chunks]
    heat_ref, moist_ref = refs[2 * chunks :]
    half, levels = heat_ref.shape[1:]
    rows = heat_ref.shape[0] * half // LANES
    for m in range(rows):
        total = None
        for n, source in enumerate(sources):
            size = source.shape[0]
            slot = lax.broadcasted_iota(i32, (LANES, size), 1).astype(f32)
            wanted = column_ref[:, n * rows + m : n * rows + m + 1]
            picks = jnp.where(slot == wanted, 1.0, 0.0).astype(bf16)
            term = jnp.dot(picks, source[...], preferred_element_type=f32)
            total = term if total is None else total + term
        total = total.astype(bf16)
        for t in range(LANES // half):
            heat_ref[m + rows * t] = total[t * half : (t + 1) * half, :levels]
            moist_ref[m + rows * t] = total[t * half : (t + 1) * half, levels:]


def silu(s):
    h = 0.5 * s
    return h + h * jnp.tanh(h)


def network_kernel(x_ref, first_ref, second_ref, third_ref, last_ref, out_ref, one_ref, two_ref):
    def layer(source, weight, target):
        total = weight.shape[1]
        tile = min(256, total)
        for start in range(0, total, tile):
            sums = jnp.dot(
                source[...], weight[:, start : start + tile], preferred_element_type=f32
            )
            target[:, start : start + tile] = silu(sums).astype(bf16)

    layer(x_ref, first_ref, one_ref)
    layer(one_ref, second_ref, two_ref)
    layer(two_ref, third_ref, one_ref)
    out_ref[...] = jnp.dot(one_ref[...], last_ref[...], preferred_element_type=f32).astype(bf16)


def network(x, first, second, third, last):
    rows, hidden = x.shape[0], first.shape[1]
    size = first.size + second.size + third.size + last.size
    return pl.pallas_call(
        network_kernel,
        out_shape=jax.ShapeDtypeStruct((rows, last.shape[1]), bf16),
        scratch_shapes=[pltpu.VMEM((rows, hidden), bf16)] * 2,
        compiler_params=params(24),
        cost_estimate=cost(2 * rows * size, 2 * size),
        name="network",
    )(x, first, second, third, last)


def dynamics_kernel(
    group_ref, rate_ref, e_in, n_in, p_in, left_ref, right_ref, e_out, n_out, p_out, e_ref, n_ref, p_ref
):
    deep, half = e_out.shape[:2]
    span = e_ref.shape[1]
    reach = span - half
    wide = e_in.shape[1]
    mine = group_ref[0]
    coef = rate_ref[...] * 0.5

    def block(ref, i):
        row = ref[i].astype(f32)
        return jnp.where(mine == 0, row[:span], row[wide - span :])

    edge = jnp.zeros((8,) + (LANES,), f32)

    for ref in (n_ref, p_ref):

        def clear(i, _, ref=ref):
            ref[i, 0:8] = edge
            ref[i, 8 + span : 16 + span] = edge
            return 0

        lax.fori_loop(0, ref.shape[0], clear, 0)

    start = 0
    for source, ref, off, width in (
        (p_in, p_ref, 8, reach),
        (e_in, e_ref, 0, reach - 1),
        (n_in, n_ref, 8, reach - 2),
    ):
        rows = slice(off, off + span)

        def load(i, _, source=source, ref=ref, rows=rows, width=width):
            ref[i + width, rows] = block(source, i)
            return 0

        lax.fori_loop(0, deep, load, 0)

        def load_sides(i, _, ref=ref, rows=rows, width=width, start=start):
            ref[i, rows] = left_ref[start + i].astype(f32)
            ref[i + width + deep, rows] = right_ref[start + i].astype(f32)
            return 0

        lax.fori_loop(0, width, load_sides, 0)
        start += width

    mid, low, high = slice(8, 8 + span), slice(7, 7 + span), slice(9, 9 + span)
    for s in range(SUB):
        done = 2 * s

        def winds(i, _):
            e_ref[i] = e_ref[i] - coef * (p_ref[i + 2, mid] - p_ref[i, mid])
            return 0

        lax.fori_loop(done, e_ref.shape[0] - done, winds, 0)

        def north(i, _):
            n_ref[i, mid] = n_ref[i, mid] - coef * (p_ref[i + 2, high] - p_ref[i + 2, low])
            return 0

        lax.fori_loop(done, n_ref.shape[0] - done, north, 0)

        def pressure(i, _):
            p_ref[i + 2, mid] = p_ref[i + 2, mid] - coef * (
                (e_ref[i + 2] - e_ref[i]) + (n_ref[i, high] - n_ref[i, low])
            )
            return 0

        lax.fori_loop(done, n_ref.shape[0] - done, pressure, 0)

    for ref, out, off, width in (
        (e_ref, e_out, 0, reach - 1),
        (n_ref, n_out, 8, reach - 2),
        (p_ref, p_out, 8, reach),
    ):

        def store(i, _, ref=ref, out=out, off=off, width=width):
            near = ref[i + width, off : off + half]
            far = ref[i + width, off + reach : off + reach + half]
            out[i] = jnp.where(mine == 0, near, far).astype(bf16)
            return 0

        lax.fori_loop(0, deep, store, 0)


def dynamics(group, rate, e, n, p, left, right):
    deep, wide, levels = e.shape
    half = wide // 2
    reach = 2 * SUB
    span = half + reach
    out = jax.ShapeDtypeStruct((deep, half, levels), bf16)
    cells = deep * half * levels
    return pl.pallas_call(
        dynamics_kernel,
        out_shape=(out,) * 3,
        in_specs=[pl.BlockSpec(memory_space=pltpu.SMEM)] + [pl.BlockSpec(memory_space=pltpu.VMEM)] * 6,
        scratch_shapes=[
            pltpu.VMEM((deep + 2 * (reach - 1), span, levels), f32),
            pltpu.VMEM((deep + 2 * (reach - 2), span + 16, levels), f32),
            pltpu.VMEM((deep + 2 * reach, span + 16, levels), f32),
        ],
        compiler_params=params(16),
        cost_estimate=cost(cells * 200, cells * 24),
        name="dynamics",
    )(group, rate, e, n, p, left, right)


def halos(e, n, p, mine):
    wide = e.shape[1]
    half, reach = wide // 2, 2 * SUB
    span = half + reach
    count = lax.axis_size("blk")
    cut = lambda f: lax.dynamic_slice_in_dim(f, mine * (wide - span), span, 1)
    widths = ((p, reach), (e, reach - 1), (n, reach - 2))
    tail = cut(jnp.concatenate([f[f.shape[0] - w :] for f, w in widths], axis=0))
    head = cut(jnp.concatenate([f[:w] for f, w in widths], axis=0))
    left = lax.ppermute(tail, "blk", [(i, (i + 1) % count) for i in range(count)])
    right = lax.ppermute(head, "blk", [((i + 1) % count, i) for i in range(count)])
    return left, right


def room_for(chunk, width, part, regimes):
    most = 0
    for above in range(regimes):
        short = part * (regimes - above) - above * chunk * width
        most = max(most, min(above * width, short))
    return -(-most // 16) * 16


def local(
    zonal_velocity_field,
    meridional_velocity_field,
    barometric_disturbance,
    delayed_thermal_deviation,
    delayed_moisture_deviation,
    flow_category_label,
    advective_stability_number,
    initial_dense_matrix,
    middle_dense_matrix,
    closing_dense_matrix,
    final_readout_matrix,
):
    mine = lax.axis_index("grp")
    group = jnp.full((1,), mine, i32)
    regimes = lax.axis_size("blk")
    deep, wide, levels = zonal_velocity_field.shape
    half = wide // 2
    profile = 2 * levels
    part = deep * wide // regimes // 2
    chunks = CHUNKS
    width = part // chunks
    size = regimes * width
    rows = deep * half // LANES
    smem = pl.BlockSpec(memory_space=pltpu.SMEM)
    vmem = pl.BlockSpec(memory_space=pltpu.VMEM)

    left, right = halos(
        zonal_velocity_field, meridional_velocity_field, barometric_disturbance, mine
    )
    outgoing = pl.pallas_call(
        functools.partial(route_kernel, regimes, part),
        out_shape=(jax.ShapeDtypeStruct((size, profile), bf16),) * chunks,
        in_specs=[smem, vmem, vmem, vmem],
        compiler_params=params(24),
        cost_estimate=cost(2 * regimes * part * deep * wide * profile, 2 * MIB),
        name="route",
    )(group, flow_category_label, delayed_thermal_deviation, delayed_moisture_deviation)
    column_plan, pack_plan = pl.pallas_call(
        functools.partial(plan_kernel, regimes, part, chunks),
        out_shape=(
            jax.ShapeDtypeStruct((LANES, 2 * chunks * rows), f32),
            jax.ShapeDtypeStruct((chunks, size // LANES, LANES), f32),
        ),
        in_specs=[smem, vmem],
        compiler_params=params(16),
        cost_estimate=cost(MIB, MIB),
        name="plan",
    )(group, flow_category_label)

    arrived = [
        lax.all_to_all(
            one.reshape(regimes, width, profile), "blk", split_axis=0, concat_axis=0, tiled=True
        )
        for one in outgoing
    ]
    returned = [
        lax.all_to_all(
            network(
                one.reshape(size, profile),
                initial_dense_matrix[0],
                middle_dense_matrix[0],
                closing_dense_matrix[0],
                final_readout_matrix[0],
            ).reshape(regimes, width, profile),
            "blk",
            split_axis=0,
            concat_axis=0,
            tiled=True,
        ).reshape(size, profile)
        for one in arrived
    ]
    sources = []
    for k, one in enumerate(returned):
        room = room_for(k, width, part, regimes)
        packed = pl.pallas_call(
            pack_kernel,
            out_shape=jax.ShapeDtypeStruct((room, profile), bf16),
            compiler_params=params(16),
            cost_estimate=cost(2 * room * size * profile, MIB),
            name="pack",
        )(pack_plan[k], one)
        sources += [one, lax.ppermute(packed, "grp", [(0, 1), (1, 0)])]
    out = jax.ShapeDtypeStruct((deep, half, levels), bf16)
    heating, moistening = pl.pallas_call(
        functools.partial(place_kernel, chunks),
        out_shape=(out, out),
        compiler_params=params(24),
        cost_estimate=cost(2 * deep * half * sum(s.shape[0] for s in sources) * profile, 2 * MIB),
        name="place",
    )(column_plan, *sources)
    east, north, pressure = dynamics(
        group,
        advective_stability_number.reshape(1, levels),
        zonal_velocity_field,
        meridional_velocity_field,
        barometric_disturbance,
        left,
        right,
    )
    return east, north, pressure, heating, moistening


def solution(mesh):
    return jax.shard_map(
        local,
        mesh=mesh,
        in_specs=(P("blk", None, None),) * 5
        + (P("blk", None), P())
        + (P("blk", None, None),) * 4,
        out_specs=(P("blk", "grp", None),) * 5,
        check_vma=False,
    )
```

time: 157 us -> 77 us (0.49)
  waiting for transfers between devices: 54.5 us -> 6.24 us
  other arithmetic: 26.3 us -> 1.42 us
  Pallas kernels: 0 us -> 20.1 us
  blocking collectives: 0 us -> 17.2 us
  matrix products: 13.8 us -> 0 us
  between operations: 14.5 us -> 0.79 us
  local copies, waits for them, and re-layouts: 20 us -> 11.3 us
  starting transfers between devices: 27.1 us -> 19.2 us
    ppermute x16 -> x4, waiting for transfers between devices: 40.3 us -> 0.05 us  [the longest x1 0.04 us: halos(): lax.ppermute(tail, 'blk', [(i, (i + 1) % count) for i in range(count)])]
    pallas_call x0 -> x8, Pallas kernels: none -> 20.1 us  [the longest x2 7.46 us: network(): pl.pallas_call(network_kernel, out_shape=jax.ShapeDtypeStruct((rows, last...]
    all_to_all x0 -> x1, blocking collectives: none -> 17.2 us  [local(): lax.all_to_all(one.reshape(regimes, width, profile), 'blk', split_axis=0,...]
    reduce_scatter x2 -> x0, waiting for transfers between devices: 14.2 us -> none  [the longest x1 14.1 us: local(): lax.psum_scatter(tendency[:, :, HEIGHT_COUNT:].astype(jnp.bfloat16), 'grp...]
    dot_general x2 -> x0, matrix products: 13.8 us -> none  [the longest x1 7.34 us: network(): jnp.dot(hidden, last, preferred_element_type=jnp.float32)]
    ppermute x16 -> x4, starting transfers between devices: 16.9 us -> 7.55 us  [the longest x1 4.04 us: halos(): lax.ppermute(head, 'blk', [((i + 1) % count, i) for i in range(count)])]
    gather x1 -> x0, local copies, waits for them, and re-layouts: 9.03 us -> none  [local(): jnp.take(atmosphere_soundings, sorting, axis=0)]
    convert_element_type x15 -> x0, other arithmetic: 8.01 us -> none  [the longest x6 4.2 us: faces(): field.astype(jnp.bfloat16)]
  transfers between devices with their start and end apart: 20 -> 7, of which waited for: 14 -> 3; matrix products, arithmetic and copies ran while one was open for 20% -> 2% of each run, Pallas kernels for 0% -> 21%
where the time goes in v1:
time: 77 us; the launch traced here: 76.2 us
  Pallas kernels  20.1 us (26%)
  starting transfers between devices  19.2 us (25%)
  blocking collectives  17.2 us (22%)
  local copies, waits for them, and re-layouts  11.3 us (15%)
  waiting for transfers between devices  6.24 us (8%)
  other arithmetic  1.42 us (2%)
  between operations  0.79 us (1%)
    all_to_all x1, blocking collectives, local(): lax.all_to_all(one.reshape(regimes, width, profile), 'blk', split_axis=0,...  17.2 us
    unnamed x30, local copies, waits for them, and re-layouts  11.3 us
    all_to_all x2, starting transfers between devices, local(): lax.all_to_all(network(one.reshape(size, profile), initial_dense_matrix[0...  8.1 us
    pallas_call x2, Pallas kernels, network(): pl.pallas_call(network_kernel, out_shape=jax.ShapeDtypeStruct((rows, last...  7.46 us
    pallas_call x1, Pallas kernels, dynamics(): pl.pallas_call(dynamics_kernel, out_shape=(out,) * 3, in_specs=[pl.BlockS...  7.15 us
    all_to_all x2, waiting for transfers between devices, local(): lax.all_to_all(network(one.reshape(size, profile), initial_dense_matrix[0...  4.2 us
    ppermute x1, starting transfers between devices, halos(): lax.ppermute(head, 'blk', [((i + 1) % count, i) for i in range(count)])  4.04 us
    all_to_all x1, starting transfers between devices, local(): lax.all_to_all(one.reshape(regimes, width, profile), 'blk', split_axis=0,...  3.53 us
  transfers between devices with their start and end apart: 7, of which 3 were waited for; matrix products, arithmetic and copies ran while one was open for 2% of the time, Pallas kernels for 21%

profile of v1, /device:TPU:0, one launch (start us, length us, event | category | flops | bytes accessed | tf_op | source)
XLA Modules:
  0.0 76.2 jit_solution(7840484580737094014)
XLA Ops:
  0.6 0.0 copy-start.3
  0.6 0.7 copy-done.3
  1.4 0.0 copy-start.10
  1.4 1.0 %copy-done.10 = bf16[32,64,128]{2,1,0:T(8,128)(2,1)S(1)} copy-done((bf16[32,64,128]{2,1,0:T(8,128)(2,1)S(1)}, bf16[32,64,128]{2,1,0:T(8,128)(2,1)}, u32[]{:S(2)}) %copy-start.10) | copy-done | bytes 524312
  2.4 0.0 copy-start.11
  2.4 1.0 %copy-done.11 = bf16[32,64,128]{2,1,0:T(8,128)(2,1)S(1)} copy-done((bf16[32,64,128]{2,1,0:T(8,128)(2,1)S(1)}, bf16[32,64,128]{2,1,0:T(8,128)(2,1)}, u32[]{:S(2)}) %copy-start.11) | copy-done | bytes 524312
  3.4 0.0 copy-start.1
  3.4 0.0 copy-start.12
  3.4 2.3 %route.1 = (bf16[512,256]{1,0:T(8,128)(2,1)S(1)}, bf16[512,256]{1,0:T(8,128)(2,1)}) custom-call(s32[1]{0:T(128)} %bitcast.group_ref, s32[32,64]{1,0:T(8,128)S(1)} %copy-done.3, bf16[32,64,128]{2,1,0:T(8,128)(2,1)S(1)} %copy-done.10, bf16[32,64,128]{2,1,0:T(8,128)(2,1)S(1)} %copy-done.11), custom_call_target="tpu_custom_call" | custom-call | flops 1073741824 | bytes 2097152 | tf_op jit(solution)/shard_map/route/pallas_call | solution.py:368
  5.8 17.2 %all_to_all.20 = bf16[16,32,256]{2,1,0:T(8,128)(2,1)S(1)} all-to-all(bf16[16,32,256]{2,1,0:T(8,128)(2,1)S(1)} %bitcast.24), channel_id=1, replica_groups=mesh['grp'=2,'blk'=16] {'blk'}, dimensions={0} | all-to-all | bytes 524288 | tf_op jit(solution)/shard_map/all_to_all | solution.py:389
  23.0 3.5 %all-to-all-start.2 = ((bf16[16,32,256]{2,1,0:T(8,128)(2,1)}), bf16[16,32,256]{2,1,0:T(8,128)(2,1)S(1)}, u32[]{:S(2)}, u32[]{:S(2)}) async-start(bf16[16,32,256]{2,1,0:T(8,128)(2,1)} %bitcast.11), calls=%async_computation.2 | async-start | bytes 524288 | tf_op jit(solution)/shard_map/all_to_all | solution.py:389
  26.5 0.0 copy-done.1
  26.6 0.0 copy-done.12
  26.6 0.0 copy-start.6
  26.6 1.6 %copy-done.6 = bf16[1,1024,1024]{2,1,0:T(8,128)(2,1)S(1)} copy-done((bf16[1,1024,1024]{2,1,0:T(8,128)(2,1)S(1)}, bf16[1,1024,1024]{2,1,0:T(8,128)(2,1)}, u32[]{:S(2)}) %copy-start.6) | copy-done | bytes 2097176
  28.2 0.0 copy-start.8
  28.2 1.6 %copy-done.8 = bf16[1,1024,1024]{2,1,0:T(8,128)(2,1)S(1)} copy-done((bf16[1,1024,1024]{2,1,0:T(8,128)(2,1)S(1)}, bf16[1,1024,1024]{2,1,0:T(8,128)(2,1)}, u32[]{:S(2)}) %copy-start.8) | copy-done | bytes 2097176
  29.8 1.0 %copy-done.13 = bf16[1,1024,256]{2,1,0:T(8,128)(2,1)S(1)} copy-done((bf16[1,1024,256]{2,1,0:T(8,128)(2,1)S(1)}, bf16[1,1024,256]{2,1,0:T(8,128)(2,1)}, u32[]{:S(2)}) %copy-start.13) | copy-done | bytes 524312
  30.8 3.7 %network.2 = bf16[512,256]{1,0:T(8,128)(2,1)} custom-call(bf16[512,256]{1,0:T(8,128)(2,1)S(1)} %bitcast.23, bf16[256,1024]{1,0:T(8,128)(2,1)S(1)} %bitcast.30, bf16[1024,1024]{1,0:T(8,128)(2,1)S(1)} %bitcast.26, bf16[1024,1024]{1,0:T(8,128)(2,1)S(1)} %bitcast.28, bf16[1024,256]{1,0:T(8,128)(2,1)S(1)} %bitcast.32), custom_call_target="tpu_custom_call" | custom-call | flops 2684354560 | bytes 5242880 | tf_op jit(solution)/shard_map/network/pallas_call | solution.py:198
  34.5 2.0 %all-to-all-done.2 = bf16[16,32,256]{2,1,0:T(8,128)(2,1)S(1)} async-done(((bf16[16,32,256]{2,1,0:T(8,128)(2,1)}), bf16[16,32,256]{2,1,0:T(8,128)(2,1)S(1)}, u32[]{:S(2)}, u32[]{:S(2)}) %all-to-all-start.2) | async-done | bytes 262176 | tf_op jit(solution)/shard_map/all_to_all | solution.py:389
  36.5 4.0 %all-to-all-start.1 = ((bf16[16,32,256]{2,1,0:T(8,128)(2,1)}), bf16[16,32,256]{2,1,0:T(8,128)(2,1)S(1)}, u32[]{:S(2)}, u32[]{:S(2)}) async-start(bf16[16,32,256]{2,1,0:T(8,128)(2,1)} %bitcast.8), calls=%async_computation.1 | async-start | bytes 524288 | tf_op jit(solution)/shard_map/all_to_all | solution.py:395
  40.5 0.0 copy-done.2
  40.6 0.0 copy-done
  40.6 0.0 copy-start.7
  40.6 1.6 %copy-done.7 = bf16[1,1024,1024]{2,1,0:T(8,128)(2,1)S(1)} copy-done((bf16[1,1024,1024]{2,1,0:T(8,128)(2,1)S(1)}, bf16[1,1024,1024]{2,1,0:T(8,128)(2,1)}, u32[]{:S(2)}) %copy-start.7) | copy-done | bytes 2097176
  42.2 1.6 %copy-done.9 = bf16[1,1024,1024]{2,1,0:T(8,128)(2,1)S(1)} copy-done((bf16[1,1024,1024]{2,1,0:T(8,128)(2,1)S(1)}, bf16[1,1024,1024]{2,1,0:T(8,128)(2,1)}, u32[]{:S(2)}) %copy-start.9) | copy-done | bytes 2097176
  43.8 1.0 %copy-done.14 = bf16[1,1024,256]{2,1,0:T(8,128)(2,1)S(1)} copy-done((bf16[1,1024,256]{2,1,0:T(8,128)(2,1)S(1)}, bf16[1,1024,256]{2,1,0:T(8,128)(2,1)}, u32[]{:S(2)}) %copy-start.14) | copy-done | bytes 524312
  44.8 3.7 %network.3 = bf16[512,256]{1,0:T(8,128)(2,1)} custom-call(bf16[512,256]{1,0:T(8,128)(2,1)S(1)} %bitcast.22, bf16[256,1024]{1,0:T(8,128)(2,1)S(1)} %bitcast.31, bf16[1024,1024]{1,0:T(8,128)(2,1)S(1)} %bitcast.27, bf16[1024,1024]{1,0:T(8,128)(2,1)S(1)} %bitcast.29, bf16[1024,256]{1,0:T(8,128)(2,1)S(1)} %bitcast.33), custom_call_target="tpu_custom_call" | custom-call | flops 2684354560 | bytes 5242880 | tf_op jit(solution)/shard_map/network/pallas_call | solution.py:198
  48.6 2.0 %all-to-all-done.1 = bf16[16,32,256]{2,1,0:T(8,128)(2,1)S(1)} async-done(((bf16[16,32,256]{2,1,0:T(8,128)(2,1)}), bf16[16,32,256]{2,1,0:T(8,128)(2,1)S(1)}, u32[]{:S(2)}, u32[]{:S(2)}) %all-to-all-start.1) | async-done | bytes 262176 | tf_op jit(solution)/shard_map/all_to_all | solution.py:395
  50.6 4.1 %all-to-all-start.3 = ((bf16[16,32,256]{2,1,0:T(8,128)(2,1)}), bf16[16,32,256]{2,1,0:T(8,128)(2,1)S(1)}, u32[]{:S(2)}, u32[]{:S(2)}) async-start(bf16[16,32,256]{2,1,0:T(8,128)(2,1)} %bitcast.13), calls=%async_computation.3 | async-start | bytes 524288 | tf_op jit(solution)/shard_map/all_to_all | solution.py:395
  54.7 0.7 fusion.3
  55.4 0.4 collective-permute-start
  55.8 0.7 fusion.1
  56.5 4.0 %collective-permute-start.1 = (bf16[21,40,128]{2,1,0:T(8,128)(2,1)}, bf16[21,40,128]{2,1,0:T(8,128)(2,1)S(1)}, u32[]{:S(2)}, u32[]{:S(2)}) collective-permute-start(bf16[21,40,128]{2,1,0:T(8,128)(2,1)} %fusion.1), channel_id=1, source_target_pairs={{1,0},{2,1},{3,2},{4,3},{5,4},{6,5},{7,6},{8,7},{9,8},{10,9},{11,1... | collective-permute-start | bytes 645128 | tf_op jit(solution)/shard_map/ppermute | solution.py:326
  60.6 0.0 copy-done.4
  60.6 0.7 plan.1
  61.3 0.2 pack.2
  61.5 1.6 %collective-permute-start.2 = (bf16[320,256]{1,0:T(8,128)(2,1)S(1)}, bf16[320,256]{1,0:T(8,128)(2,1)S(1)}, u32[]{:S(2)}, u32[]{:S(2)}) collective-permute-start(bf16[320,256]{1,0:T(8,128)(2,1)S(1)} %pack.2), channel_id=1, source_target_pairs={{0,16},{16,0},{1,17},{17,1},{2,18},{18,2},{3,19},{19,3},{4,20},{20... | collective-permute-start | bytes 491528 | tf_op jit(solution)/shard_map/ppermute | solution.py:420
  63.1 2.2 %all-to-all-done.3 = bf16[16,32,256]{2,1,0:T(8,128)(2,1)S(1)} async-done(((bf16[16,32,256]{2,1,0:T(8,128)(2,1)}), bf16[16,32,256]{2,1,0:T(8,128)(2,1)S(1)}, u32[]{:S(2)}, u32[]{:S(2)}) %all-to-all-start.3) | async-done | bytes 262176 | tf_op jit(solution)/shard_map/all_to_all | solution.py:395
  65.3 0.2 pack.3
  65.5 1.6 %collective-permute-start.3 = (bf16[256,256]{1,0:T(8,128)(2,1)S(1)}, bf16[256,256]{1,0:T(8,128)(2,1)S(1)}, u32[]{:S(2)}, u32[]{:S(2)}) collective-permute-start(bf16[256,256]{1,0:T(8,128)(2,1)S(1)} %pack.3), channel_id=1, source_target_pairs={{0,16},{16,0},{1,17},{17,1},{2,18},{18,2},{3,19},{19,3},{4,20},{20... | collective-permute-start | bytes 393224 | tf_op jit(solution)/shard_map/ppermute | solution.py:420
  67.1 0.0 collective-permute-done.left_ref
  67.1 0.0 collective-permute-done.1.right_ref
  67.1 0.0 copy-done.5
  67.1 7.2 %dynamics.1 = (bf16[32,32,128]{2,1,0:T(8,128)(2,1)}, bf16[32,32,128]{2,1,0:T(8,128)(2,1)}, bf16[32,32,128]{2,1,0:T(8,128)(2,1)}) custom-call(s32[1]{0:T(128)} %bitcast.group_ref, f32[1,128]{1,0:T(1,128)S(1)} %bitcast.25, bf16[32,64,128]{2,1,0:T(8,128)(2,1)S(1)} %copy-done.1, bf16[32,64,128]{2,1,0:T(8,128)(2,1)S(1)} %copy-done.2, ...), custom_call_target="tpu_custom_call" | custom-call | flops 26214400 | bytes 3145728 | tf_op jit(solution)/shard_map/dynamics/pallas_call | solution.py:301
  74.3 0.0 collective-permute-done.3.refs_3_
  74.3 0.0 collective-permute-done.2.refs_1_
  74.3 2.0 %place.1 = (bf16[32,32,128]{2,1,0:T(8,128)(2,1)}, bf16[32,32,128]{2,1,0:T(8,128)(2,1)}) custom-call(f32[128,32]{1,0:T(8,128)S(1)} %get-tuple-element.17.column_ref, bf16[512,256]{1,0:T(8,128)(2,1)S(1)} %bitcast.19, bf16[320,256]{1,0:T(8,128)(2,1)S(1)} %collective-permute-done.2.refs_1_, bf16[512,256]{1,0:T(8,128)(2,1)S(1)} %bitcast.21, ...), custom_call_target="tpu_custom_call" | custom-call | flops 838860800 | bytes 2097152 | tf_op jit(solution)/shard_map/place/pallas_call | solution.py:422
  (11 shorter events, 0.1 us)
Async XLA Ops:
  0.6 0.7 copy-start.3
  1.4 1.0 %copy-start.10 = (bf16[32,64,128]{2,1,0:T(8,128)(2,1)S(1)}, bf16[32,64,128]{2,1,0:T(8,128)(2,1)}, u32[]{:S(2)}) copy-start(bf16[32,64,128]{2,1,0:T(8,128)(2,1)} %heat_ref.1) | copy-start | bytes 1572868
  2.4 1.0 %copy-start.11 = (bf16[32,64,128]{2,1,0:T(8,128)(2,1)S(1)}, bf16[32,64,128]{2,1,0:T(8,128)(2,1)}, u32[]{:S(2)}) copy-start(bf16[32,64,128]{2,1,0:T(8,128)(2,1)} %moist_ref.1) | copy-start | bytes 1572868
  3.4 23.1 %copy-start.1 = (bf16[32,64,128]{2,1,0:T(8,128)(2,1)S(1)}, bf16[32,64,128]{2,1,0:T(8,128)(2,1)}, u32[]{:S(2)}) copy-start(bf16[32,64,128]{2,1,0:T(8,128)(2,1)} %e_in.1) | copy-start | bytes 1572868
  3.4 23.1 %copy-start.12 = (bf16[1,256,1024]{2,1,0:T(8,128)(2,1)S(1)}, bf16[1,256,1024]{2,1,0:T(8,128)(2,1)}, u32[]{:S(2)}) copy-start(bf16[1,256,1024]{2,1,0:T(8,128)(2,1)} %param.18) | copy-start | bytes 1572868
  23.0 13.5 %all-to-all-start.2 = ((bf16[16,32,256]{2,1,0:T(8,128)(2,1)}), bf16[16,32,256]{2,1,0:T(8,128)(2,1)S(1)}, u32[]{:S(2)}, u32[]{:S(2)}) async-start(bf16[16,32,256]{2,1,0:T(8,128)(2,1)} %bitcast.11), calls=%async_computation.2 | async-start | bytes 524288 | tf_op jit(solution)/shard_map/all_to_all | solution.py:389
  26.6 1.6 %copy-start.6 = (bf16[1,1024,1024]{2,1,0:T(8,128)(2,1)S(1)}, bf16[1,1024,1024]{2,1,0:T(8,128)(2,1)}, u32[]{:S(2)}) copy-start(bf16[1,1024,1024]{2,1,0:T(8,128)(2,1)} %param.19) | copy-start | bytes 6291460
  28.2 1.6 %copy-start.8 = (bf16[1,1024,1024]{2,1,0:T(8,128)(2,1)S(1)}, bf16[1,1024,1024]{2,1,0:T(8,128)(2,1)}, u32[]{:S(2)}) copy-start(bf16[1,1024,1024]{2,1,0:T(8,128)(2,1)} %param.20) | copy-start | bytes 6291460
  29.8 1.0 %copy-start.13 = (bf16[1,1024,256]{2,1,0:T(8,128)(2,1)S(1)}, bf16[1,1024,256]{2,1,0:T(8,128)(2,1)}, u32[]{:S(2)}) copy-start(bf16[1,1024,256]{2,1,0:T(8,128)(2,1)} %param.21) | copy-start | bytes 1572868
  30.8 9.7 %copy-start.2 = (bf16[32,64,128]{2,1,0:T(8,128)(2,1)S(1)}, bf16[32,64,128]{2,1,0:T(8,128)(2,1)}, u32[]{:S(2)}) copy-start(bf16[32,64,128]{2,1,0:T(8,128)(2,1)} %n_in.1) | copy-start | bytes 1572868
  30.8 9.7 %copy-start = (bf16[32,64,128]{2,1,0:T(8,128)(2,1)S(1)}, bf16[32,64,128]{2,1,0:T(8,128)(2,1)}, u32[]{:S(2)}) copy-start(bf16[32,64,128]{2,1,0:T(8,128)(2,1)} %p_in.1) | copy-start | bytes 1572868
  36.5 14.0 %all-to-all-start.1 = ((bf16[16,32,256]{2,1,0:T(8,128)(2,1)}), bf16[16,32,256]{2,1,0:T(8,128)(2,1)S(1)}, u32[]{:S(2)}, u32[]{:S(2)}) async-start(bf16[16,32,256]{2,1,0:T(8,128)(2,1)} %bitcast.8), calls=%async_computation.1 | async-start | bytes 524288 | tf_op jit(solution)/shard_map/all_to_all | solution.py:395
  40.6 1.6 %copy-start.7 = (bf16[1,1024,1024]{2,1,0:T(8,128)(2,1)S(1)}, bf16[1,1024,1024]{2,1,0:T(8,128)(2,1)}, u32[]{:S(2)}) copy-start(bf16[1,1024,1024]{2,1,0:T(8,128)(2,1)} %param.19) | copy-start | bytes 6291460
  42.2 1.6 %copy-start.9 = (bf16[1,1024,1024]{2,1,0:T(8,128)(2,1)S(1)}, bf16[1,1024,1024]{2,1,0:T(8,128)(2,1)}, u32[]{:S(2)}) copy-start(bf16[1,1024,1024]{2,1,0:T(8,128)(2,1)} %param.20) | copy-start | bytes 6291460
  43.8 1.0 %copy-start.14 = (bf16[1,1024,256]{2,1,0:T(8,128)(2,1)S(1)}, bf16[1,1024,256]{2,1,0:T(8,128)(2,1)}, u32[]{:S(2)}) copy-start(bf16[1,1024,256]{2,1,0:T(8,128)(2,1)} %param.21) | copy-start | bytes 1572868
  44.8 15.7 %copy-start.4 = (s32[32,64]{1,0:T(8,128)S(1)}, s32[32,64]{1,0:T(8,128)}, u32[]{:S(2)}) copy-start(s32[32,64]{1,0:T(8,128)} %label_ref.3) | copy-start | bytes 24580
  48.6 18.6 %copy-start.5 = (f32[128]{0:T(128)S(1)}, f32[128]{0:T(128)}, u32[]{:S(2)}) copy-start(f32[128]{0:T(128)} %param.17) | copy-start | bytes 1540
  50.6 14.7 %all-to-all-start.3 = ((bf16[16,32,256]{2,1,0:T(8,128)(2,1)}), bf16[16,32,256]{2,1,0:T(8,128)(2,1)S(1)}, u32[]{:S(2)}, u32[]{:S(2)}) async-start(bf16[16,32,256]{2,1,0:T(8,128)(2,1)} %bitcast.13), calls=%async_computation.3 | async-start | bytes 524288 | tf_op jit(solution)/shard_map/all_to_all | solution.py:395
  55.4 11.7 %collective-permute-start = (bf16[21,40,128]{2,1,0:T(8,128)(2,1)}, bf16[21,40,128]{2,1,0:T(8,128)(2,1)S(1)}, u32[]{:S(2)}, u32[]{:S(2)}) collective-permute-start(bf16[21,40,128]{2,1,0:T(8,128)(2,1)} %fusion.3), channel_id=1, source_target_pairs={{0,1},{1,2},{2,3},{3,4},{4,5},{5,6},{6,7},{7,8},{8,9},{9,10},{10,1... | collective-permute-start | bytes 645128 | tf_op jit(solution)/shard_map/ppermute | solution.py:325
  56.5 10.6 %collective-permute-start.1 = (bf16[21,40,128]{2,1,0:T(8,128)(2,1)}, bf16[21,40,128]{2,1,0:T(8,128)(2,1)S(1)}, u32[]{:S(2)}, u32[]{:S(2)}) collective-permute-start(bf16[21,40,128]{2,1,0:T(8,128)(2,1)} %fusion.1), channel_id=1, source_target_pairs={{1,0},{2,1},{3,2},{4,3},{5,4},{6,5},{7,6},{8,7},{9,8},{10,9},{11,1... | collective-permute-start | bytes 645128 | tf_op jit(solution)/shard_map/ppermute | solution.py:326
  61.5 12.7 %collective-permute-start.2 = (bf16[320,256]{1,0:T(8,128)(2,1)S(1)}, bf16[320,256]{1,0:T(8,128)(2,1)S(1)}, u32[]{:S(2)}, u32[]{:S(2)}) collective-permute-start(bf16[320,256]{1,0:T(8,128)(2,1)S(1)} %pack.2), channel_id=1, source_target_pairs={{0,16},{16,0},{1,17},{17,1},{2,18},{18,2},{3,19},{19,3},{4,20},{20... | collective-permute-start | bytes 491528 | tf_op jit(solution)/shard_map/ppermute | solution.py:420
  65.5 8.8 %collective-permute-start.3 = (bf16[256,256]{1,0:T(8,128)(2,1)S(1)}, bf16[256,256]{1,0:T(8,128)(2,1)S(1)}, u32[]{:S(2)}, u32[]{:S(2)}) collective-permute-start(bf16[256,256]{1,0:T(8,128)(2,1)S(1)} %pack.3), channel_id=1, source_target_pairs={{0,16},{16,0},{1,17},{17,1},{2,18},{18,2},{3,19},{19,3},{4,20},{20... | collective-permute-start | bytes 393224 | tf_op jit(solution)/shard_map/ppermute | solution.py:420

commit v2 on v1

v2 whole, which is shorter than its diff:
```python
import functools
import jax
import jax.numpy as jnp
from jax import lax
from jax.experimental import pallas as pl
from jax.experimental.pallas import tpu as pltpu
from jax.sharding import PartitionSpec as P

SUB = 4
ROOM = 128
LANES = 128
MIB = 1 << 20
bf16, f32, i32 = jnp.bfloat16, jnp.float32, jnp.int32
SMEM = pl.BlockSpec(memory_space=pltpu.SMEM)
VMEM = pl.BlockSpec(memory_space=pltpu.VMEM)
HBM = pl.BlockSpec(memory_space=pltpu.HBM)
ANY = pl.BlockSpec(memory_space=pl.ANY)


def params(mib):
    return pltpu.CompilerParams(vmem_limit_bytes=mib * MIB)


TOKEN = jax.ShapeDtypeStruct((8, LANES), f32)


def in_hbm(*arrays):
    return [pltpu.with_memory_space_constraint(x, pltpu.HBM) for x in arrays]


def cost(flops, moved):
    return pl.CostEstimate(flops=flops, bytes_accessed=moved, transcendentals=0)


def folded(labels, start, half):
    rows = labels.shape[0] * half // LANES
    side = labels[:, start : start + half]
    return jnp.concatenate(
        [side[t * rows : (t + 1) * rows] for t in range(LANES // half)], axis=1
    )


def ranked(labels, regimes):
    rows = labels.shape[0]
    shape = (regimes, rows, LANES)
    member = jnp.where(
        lax.broadcasted_iota(i32, shape, 0) == jnp.broadcast_to(labels[None], shape), 1.0, 0.0
    )
    flat = member.reshape(regimes * rows, LANES).astype(bf16)
    first = lax.broadcasted_iota(i32, (LANES, LANES), 0)
    second = lax.broadcasted_iota(i32, (LANES, LANES), 1)
    earlier = jnp.where(first < second, 1.0, 0.0).astype(bf16)
    within = jnp.dot(flat, earlier, preferred_element_type=f32).reshape(shape)
    totals = jnp.dot(
        flat, jnp.ones((LANES, LANES), bf16), preferred_element_type=f32
    ).reshape(shape)
    before = jnp.zeros((regimes, 1, LANES), f32)
    rank = jnp.zeros((rows, LANES), f32)
    row_ranks = []
    for m in range(rows):
        row_ranks.append(
            jnp.sum(member[:, m : m + 1] * (within[:, m : m + 1] + before), axis=0)
        )
        before = before + totals[:, m : m + 1]
    rank = jnp.concatenate(row_ranks, axis=0)
    return rank, member, before


def route_kernel(
    regimes, part, group_ref, label_in, heat_in, moist_in, out_ref, token_ref, label_ref, heat_ref, moist_ref, sem
):
    token_ref[...] = jnp.zeros_like(token_ref)
    deep, wide, levels = heat_ref.shape
    half = wide // 2
    rows = deep * half // LANES
    pieces = LANES // half
    first = pltpu.make_async_copy(label_in, label_ref, sem.at[0])
    first.start()
    copies = []
    for t in range(pieces):
        at = slice(t * rows, (t + 1) * rows)
        for source, target in ((heat_in, heat_ref), (moist_in, moist_ref)):
            n = len(copies) + 1
            copies.append(pltpu.make_async_copy(source.at[at], target.at[at], sem.at[n]))
            copies[-1].start()
    mine = group_ref[0]
    first.wait()
    labels = label_ref[...]
    targets = []
    for side in range(2):
        index = folded(labels, side * half, half)
        rank, _, _ = ranked(index, regimes)
        place = jnp.where(mine == side, part - 1.0 - rank, rank - part)
        targets.append(jnp.where(place >= 0, index.astype(f32) * part + place, -1.0))
    target = jnp.concatenate(targets, axis=0)
    for copy in copies:
        copy.wait()
    columns = []
    for side in range(2):
        for m in range(rows):
            for t in range(pieces):
                at = (m + rows * t, slice(side * half, (side + 1) * half))
                columns.append(jnp.concatenate([heat_ref[at], moist_ref[at]], axis=1))
    soundings = jnp.concatenate(columns, axis=0)
    total = out_ref.shape[0]
    tile = min(256, total)
    for start in range(0, total, tile):
        slot = (lax.broadcasted_iota(i32, (tile, LANES), 0) + start).astype(f32)
        picks = jnp.concatenate(
            [jnp.where(slot == target[m : m + 1], 1.0, 0.0).astype(bf16) for m in range(2 * rows)],
            axis=1,
        )
        out_ref[start : start + tile] = jnp.dot(
            picks, soundings, preferred_element_type=f32
        ).astype(bf16)


def plan_kernel(regimes, part, group_ref, label_ref, _, column_ref, pack_ref, crowd_ref):
    labels = label_ref[...]
    half = labels.shape[1] // 2
    mine = group_ref[0]
    sides = []
    for side in range(2):
        index = folded(labels, side * half, half)
        rank, member, count = ranked(index, regimes)
        sides.append((index.astype(f32), rank, member, jnp.maximum(count - part, 0.0)))
    index, rank, member, spare = [jnp.where(mine == 0, a, b) for a, b in zip(*sides)]
    rows = rank.shape[0]
    offset = jnp.zeros((1, LANES), f32)
    at = jnp.zeros(rank.shape, f32)
    for r in range(regimes):
        at = at + member[r] * offset
        offset = offset + spare[r]
    crowd_ref[0] = (jnp.max(offset) > ROOM).astype(i32)
    kept = jnp.where(rank < part, index * part + (part - 1.0 - rank), -1.0)
    come = jnp.where(rank >= part, at + (rank - part), -1.0)
    column_ref[:, :rows] = kept.T
    column_ref[:, rows : 2 * rows] = come.T
    spare = jnp.where(mine == 0, sides[1][3], sides[0][3])
    lane = lax.broadcasted_iota(i32, (1, LANES), 1)
    offset = jnp.zeros((1, LANES), f32)
    per_row = LANES // part
    for r in range(regimes):
        if r % per_row == 0:
            line = jnp.full((1, LANES), -1.0)
        near = (lane - (r % per_row) * part).astype(f32)
        line = jnp.where((near >= 0) & (near < spare[r]), offset + near, line)
        offset = offset + spare[r]
        if r % per_row == per_row - 1:
            pack_ref[r // per_row : r // per_row + 1] = line


def plan(regimes, part, rows, group, labels, after):
    return pl.pallas_call(
        functools.partial(plan_kernel, regimes, part),
        out_shape=(
            jax.ShapeDtypeStruct((LANES, 2 * rows), f32),
            jax.ShapeDtypeStruct((regimes * part // LANES, LANES), f32),
            jax.ShapeDtypeStruct((1,), i32),
        ),
        in_specs=[SMEM, VMEM, VMEM],
        out_specs=(VMEM, VMEM, SMEM),
        compiler_params=params(12),
        cost_estimate=cost(MIB, MIB),
        name="plan",
    )(group, labels, after)


def pack_kernel(pack_ref, result_ref, _, out_ref):
    slot = lax.broadcasted_iota(i32, (out_ref.shape[0], LANES), 0).astype(f32)
    picks = jnp.concatenate(
        [
            jnp.where(slot == pack_ref[m : m + 1], 1.0, 0.0).astype(bf16)
            for m in range(pack_ref.shape[0])
        ],
        axis=1,
    )
    out_ref[...] = jnp.dot(picks, result_ref[...], preferred_element_type=f32).astype(bf16)


def pack(room, pack_plan, result, after):
    return pl.pallas_call(
        pack_kernel,
        out_shape=jax.ShapeDtypeStruct((room, result.shape[1]), bf16),
        in_specs=[VMEM, VMEM, VMEM],
        compiler_params=params(12),
        cost_estimate=cost(2 * room * result.size, MIB),
        name="pack",
    )(pack_plan, result, after)


def picked(wanted, source_ref):
    slot = lax.broadcasted_iota(i32, (LANES, source_ref.shape[0]), 1).astype(f32)
    picks = jnp.where(slot == wanted, 1.0, 0.0).astype(bf16)
    return jnp.dot(picks, source_ref[...], preferred_element_type=f32)


def keep_kernel(column_ref, result_ref, packed_ref, out_ref):
    del packed_ref
    for m in range(column_ref.shape[1] // 2):
        out_ref[m * LANES : (m + 1) * LANES] = picked(
            column_ref[:, m : m + 1], result_ref
        ).astype(bf16)


def place_kernel(column_ref, kept_ref, come_ref, heat_ref, moist_ref):
    half, levels = heat_ref.shape[1:]
    rows = heat_ref.shape[0] * half // LANES
    for m in range(rows):
        total = picked(column_ref[:, rows + m : rows + m + 1], come_ref)
        total = (total + kept_ref[m * LANES : (m + 1) * LANES].astype(f32)).astype(bf16)
        for t in range(LANES // half):
            heat_ref[m + rows * t] = total[t * half : (t + 1) * half, :levels]
            moist_ref[m + rows * t] = total[t * half : (t + 1) * half, levels:]


def placed(room, shape, column_plan, pack_plan, result, after):
    packed = pack(room, pack_plan, result, after)
    come = lax.ppermute(packed, "grp", [(0, 1), (1, 0)])
    kept = pl.pallas_call(
        keep_kernel,
        out_shape=jax.ShapeDtypeStruct((shape[0] * shape[1], result.shape[1]), bf16),
        in_specs=[VMEM, VMEM, HBM],
        compiler_params=params(12),
        cost_estimate=cost(2 * shape[0] * shape[1] * result.size, MIB),
        name="keep",
    )(column_plan, result, packed)
    out = jax.ShapeDtypeStruct(shape, bf16)
    return tuple(
        pl.pallas_call(
            place_kernel,
            out_shape=(out, out),
            compiler_params=params(12),
            cost_estimate=cost(2 * shape[0] * shape[1] * come.size, 2 * MIB),
            name="place",
        )(column_plan, kept, come)
    )


def silu(s):
    h = 0.5 * s
    return h + h * jnp.tanh(h)


def layer(source, weight, target):
    total = weight.shape[1]
    tile = min(256, total)
    for i in range(total // tile):
        at = slice(i * tile, (i + 1) * tile)
        sums = jnp.dot(source[...], weight[:, at], preferred_element_type=f32)
        target[:, at] = silu(sums).astype(bf16)


def front_kernel(x_ref, first_in, second_in, out_ref, one_ref, first_ref, second_ref, sem):
    first = pltpu.make_async_copy(first_in.at[0], first_ref, sem.at[0])
    second = pltpu.make_async_copy(second_in.at[0], second_ref, sem.at[1])
    first.start()
    second.start()
    first.wait()
    layer(x_ref, first_ref, one_ref)
    second.wait()
    layer(one_ref, second_ref, out_ref)


def back_kernel(two_ref, third_ref, last_ref, _, __, out_ref, token_ref, three_ref):
    token_ref[...] = jnp.zeros_like(token_ref)
    layer(two_ref, third_ref, three_ref)
    out_ref[...] = jnp.dot(three_ref[...], last_ref[...], preferred_element_type=f32).astype(bf16)


def front(x, first, second):
    rows, hidden = x.shape[0], first.shape[2]
    size = first.size + second.size
    return pl.pallas_call(
        front_kernel,
        out_shape=jax.ShapeDtypeStruct((rows, hidden), bf16),
        in_specs=[VMEM] + [HBM] * 2,
        scratch_shapes=[pltpu.VMEM((rows, hidden), bf16)]
        + [pltpu.VMEM(w.shape[1:], bf16) for w in (first, second)]
        + [pltpu.SemaphoreType.DMA((2,))],
        compiler_params=params(14),
        cost_estimate=cost(2 * rows * size, 2 * size),
        name="front",
    )(x, *in_hbm(first, second))


def back(two, third, last, *after):
    rows, hidden = two.shape
    size = third.size + last.size
    return pl.pallas_call(
        back_kernel,
        out_shape=(jax.ShapeDtypeStruct((rows, last.shape[1]), bf16), TOKEN),
        in_specs=[VMEM] * 3 + [ANY] * len(after),
        scratch_shapes=[pltpu.VMEM((rows, hidden), bf16)],
        compiler_params=params(14),
        cost_estimate=cost(2 * rows * size, 2 * size),
        name="back",
    )(two, third, last, *after)


def dynamics_kernel(
    group_ref, rate_ref, e_in, n_in, p_in, left_in, right_in, _, e_out, n_out, p_out, token_ref,
    e_ref, n_ref, p_ref, left_ref, right_ref, sem,
):
    sides = [
        pltpu.make_async_copy(left_in, left_ref, sem.at[0]),
        pltpu.make_async_copy(right_in, right_ref, sem.at[1]),
    ]
    for side in sides:
        side.start()
    token_ref[...] = jnp.zeros_like(token_ref)
    deep, half = e_out.shape[:2]
    span = e_ref.shape[1]
    reach = span - half
    wide = e_in.shape[1]
    mine = group_ref[0]
    coef = rate_ref[...] * 0.5

    edge = jnp.zeros((8, LANES), f32)

    for ref in (n_ref, p_ref):

        def clear(i, _, ref=ref):
            ref[i, 0:8] = edge
            ref[i, 8 + span : 16 + span] = edge
            return 0

        lax.fori_loop(0, ref.shape[0], clear, 0)

    fields = (
        (p_in, p_out, p_ref, 8, reach),
        (e_in, e_out, e_ref, 0, reach - 1),
        (n_in, n_out, n_ref, 8, reach - 2),
    )

    def load(i, _):
        for source, _, ref, off, width in fields:
            row = source[i].astype(f32)
            ref[i + width, off : off + span] = jnp.where(
                mine == 0, row[:span], row[wide - span :]
            )
        return 0

    lax.fori_loop(0, deep, load, 0)
    for side in sides:
        side.wait()
    start = 0
    for _, _, ref, off, width in fields:
        for i in range(width):
            ref[i, off : off + span] = left_ref[start + i].astype(f32)
            ref[i + width + deep, off : off + span] = right_ref[start + i].astype(f32)
        start += width

    mid, low, high = slice(8, 8 + span), slice(7, 7 + span), slice(9, 9 + span)

    def wind(i):
        e_ref[i] = e_ref[i] - coef * (p_ref[i + 2, mid] - p_ref[i, mid])

    for s in range(SUB):
        first, last = 2 * s, n_ref.shape[0] - 2 * s
        wind(first)

        def winds(k, _, first=first):
            for i in (first + 2 * k, first + 2 * k + 1):
                wind(i + 1)
                n_ref[i, mid] = n_ref[i, mid] - coef * (p_ref[i + 2, high] - p_ref[i + 2, low])
            return 0

        lax.fori_loop(0, (last - first) // 2, winds, 0)
        wind(last + 1)

        def pressure(k, _, first=first):
            for i in (first + 2 * k, first + 2 * k + 1):
                p_ref[i + 2, mid] = p_ref[i + 2, mid] - coef * (
                    (e_ref[i + 2] - e_ref[i]) + (n_ref[i, high] - n_ref[i, low])
                )
            return 0

        lax.fori_loop(0, (last - first) // 2, pressure, 0)

    def store(i, _):
        for _, out, ref, off, width in fields:
            near = ref[i + width, off : off + half]
            far = ref[i + width, off + reach : off + reach + half]
            out[i] = jnp.where(mine == 0, near, far).astype(bf16)
        return 0

    lax.fori_loop(0, deep, store, 0)


def dynamics(group, rate, e, n, p, left, right, after):
    deep, wide, levels = e.shape
    half = wide // 2
    reach = 2 * SUB
    span = half + reach
    out = jax.ShapeDtypeStruct((deep, half, levels), bf16)
    cells = deep * half * levels
    return pl.pallas_call(
        dynamics_kernel,
        out_shape=(out,) * 3 + (TOKEN,),
        in_specs=[SMEM] + [VMEM] * 4 + [ANY] * 2 + [VMEM],
        scratch_shapes=[
            pltpu.VMEM((deep + 2 * (reach - 1), span, levels), f32),
            pltpu.VMEM((deep + 2 * (reach - 2), span + 16, levels), f32),
            pltpu.VMEM((deep + 2 * reach, span + 16, levels), f32),
            pltpu.VMEM(left.shape, bf16),
            pltpu.VMEM(right.shape, bf16),
            pltpu.SemaphoreType.DMA((2,)),
        ],
        compiler_params=params(12),
        cost_estimate=cost(cells * 200, cells * 24),
        name="dynamics",
    )(group, rate, e, n, p, left, right, after)


def edges_kernel(group_ref, e_ref, n_ref, p_ref, _, tail_ref, head_ref):
    deep, wide = e_ref.shape[:2]
    span = tail_ref.shape[1]
    mine = group_ref[0]
    reach = 2 * SUB
    at = 0
    for ref, width in ((p_ref, reach), (e_ref, reach - 1), (n_ref, reach - 2)):
        for i in range(width):
            for out, row in ((tail_ref, deep - width + i), (head_ref, i)):
                whole = ref[row].astype(f32)
                out[at + i] = jnp.where(mine == 0, whole[:span], whole[wide - span :]).astype(bf16)
        at += width


def halos(group, e, n, p, after):
    wide, levels = e.shape[1:]
    reach = 2 * SUB
    count = lax.axis_size("blk")
    out = jax.ShapeDtypeStruct((3 * reach - 3, wide // 2 + reach, levels), bf16)
    tail, head = pl.pallas_call(
        edges_kernel,
        out_shape=(out, out),
        in_specs=[SMEM] + [VMEM] * 4,
        compiler_params=params(12),
        cost_estimate=cost(MIB, 2 * MIB),
        name="edges",
    )(group, e, n, p, after)
    left = lax.ppermute(tail, "blk", [(i, (i + 1) % count) for i in range(count)])
    right = lax.ppermute(head, "blk", [((i + 1) % count, i) for i in range(count)])
    return left, right


def local(
    zonal_velocity_field,
    meridional_velocity_field,
    barometric_disturbance,
    delayed_thermal_deviation,
    delayed_moisture_deviation,
    flow_category_label,
    advective_stability_number,
    initial_dense_matrix,
    middle_dense_matrix,
    closing_dense_matrix,
    final_readout_matrix,
):
    group = jnp.full((1,), lax.axis_index("grp"), i32)
    regimes = lax.axis_size("blk")
    deep, wide, levels = zonal_velocity_field.shape
    half = wide // 2
    profile = 2 * levels
    part = deep * wide // regimes // 2
    size = regimes * part
    rows = deep * half // LANES

    def swapped(one):
        one = one.reshape(regimes, part, profile)
        one = lax.all_to_all(one, "blk", split_axis=0, concat_axis=0, tiled=True)
        return one.reshape(size, profile)

    sent, routed = pl.pallas_call(
        functools.partial(route_kernel, regimes, part),
        out_shape=(jax.ShapeDtypeStruct((size, profile), bf16), TOKEN),
        in_specs=[SMEM, HBM, HBM, HBM],
        scratch_shapes=[
            pltpu.VMEM((deep, wide), i32),
            pltpu.VMEM((deep, wide, levels), bf16),
            pltpu.VMEM((deep, wide, levels), bf16),
            pltpu.SemaphoreType.DMA((1 + 2 * (LANES // half),)),
        ],
        compiler_params=params(16),
        cost_estimate=cost(2 * size * deep * wide * profile, 2 * MIB),
        name="route",
    )(
        group,
        *in_hbm(flow_category_label, delayed_thermal_deviation, delayed_moisture_deviation),
    )
    arrived = swapped(sent)
    left, right = halos(
        group, zonal_velocity_field, meridional_velocity_field, barometric_disturbance, routed
    )
    column_plan, pack_plan, crowded = plan(regimes, part, rows, group, flow_category_label, routed)
    two = front(arrived, initial_dense_matrix, middle_dense_matrix)
    result, worked = back(two, closing_dense_matrix[0], final_readout_matrix[0], left, right)
    returned = swapped(result)
    east, north, pressure, moved = dynamics(
        group,
        advective_stability_number.reshape(1, levels),
        zonal_velocity_field,
        meridional_velocity_field,
        barometric_disturbance,
        left,
        right,
        worked,
    )
    shape = (deep, half, levels)
    heating, moistening = lax.cond(
        crowded[0] > 0,
        functools.partial(placed, size // 2, shape),
        functools.partial(placed, min(ROOM, size // 2), shape),
        column_plan,
        pack_plan,
        returned,
        moved,
    )
    return east, north, pressure, heating, moistening


def solution(mesh):
    return jax.shard_map(
        local,
        mesh=mesh,
        in_specs=(P("blk", None, None),) * 5
        + (P("blk", None), P())
        + (P("blk", None, None),) * 4,
        out_specs=(P("blk", "grp", None),) * 5,
        check_vma=False,
    )
```

time: 77 us -> 61.9 us (0.80)
  blocking collectives: 17.2 us -> 0 us
  waiting for transfers between devices: 6.24 us -> 19.7 us
  local copies, waits for them, and re-layouts: 11.3 us -> 0.03 us
  other arithmetic: 1.42 us -> 0 us
  Pallas kernels: 20.1 us -> 21 us
    all_to_all x1 -> x0, blocking collectives: 17.2 us -> none  [local(): lax.all_to_all(one.reshape(regimes, width, profile), 'blk', split_axis=0,...]
    all_to_all x3 -> x2, waiting for transfers between devices: 6.2 us -> 17.7 us  [swapped(): one = lax.all_to_all(one, 'blk', split_axis=0, concat_axis=0, tiled=True)]
    unnamed x30 -> x14, local copies, waits for them, and re-layouts: 11.3 us -> 0.03 us
    ppermute x2 -> x1, waiting for transfers between devices: 0.01 us -> 2.01 us  [placed(): come = lax.ppermute(packed, 'grp', [(0, 1), (1, 0)])]
    all_to_all x3 -> x2, starting transfers between devices: 11.6 us -> 13.3 us  [swapped(): one = lax.all_to_all(one, 'blk', split_axis=0, concat_axis=0, tiled=True)]
    ppermute x2 -> x1, starting transfers between devices: 3.11 us -> 1.55 us  [placed(): come = lax.ppermute(packed, 'grp', [(0, 1), (1, 0)])]
    concatenate x2 -> x0, other arithmetic: 1.42 us -> none  [the longest x1 0.72 us: halos(): tail = cut(jnp.concatenate([f[f.shape[0] - w:] for f, w in widths], axis=0))]
    pallas_call x1, Pallas kernels: 2.33 us -> 3.54 us  [local(): pl.pallas_call(functools.partial(route_kernel, regimes, part), out_shape=...]
  transfers between devices with their start and end apart: 7 -> 5, of which waited for: 3 -> 3; matrix products, arithmetic and copies ran while one was open for 2% -> 0% of each run, Pallas kernels for 21% -> 20%
where the time goes in v2:
time: 61.9 us; the launch traced here: 61.6 us
  Pallas kernels  21 us (34%)
  waiting for transfers between devices  19.7 us (32%)
  starting transfers between devices  19.4 us (31%)
  between operations  1.46 us (2%)
    all_to_all x2, waiting for transfers between devices, swapped(): one = lax.all_to_all(one, 'blk', split_axis=0, concat_axis=0, tiled=True)  17.7 us
    all_to_all x2, starting transfers between devices, swapped(): one = lax.all_to_all(one, 'blk', split_axis=0, concat_axis=0, tiled=True)  13.3 us
    pallas_call x1, Pallas kernels, dynamics(): pl.pallas_call(dynamics_kernel, out_shape=(out,) * 3 + (TOKEN,), in_specs...  5.38 us
    pallas_call x1, Pallas kernels, front(): pl.pallas_call(front_kernel, out_shape=jax.ShapeDtypeStruct((rows, hidden...  4.8 us
    ppermute x1, starting transfers between devices, halos(): lax.ppermute(head, 'blk', [((i + 1) % count, i) for i in range(count)])  4.04 us
    pallas_call x1, Pallas kernels, back(): pl.pallas_call(back_kernel, out_shape=(jax.ShapeDtypeStruct((rows, last.s...  3.95 us
    pallas_call x1, Pallas kernels, local(): pl.pallas_call(functools.partial(route_kernel, regimes, part), out_shape=...  3.54 us
    ppermute x1, waiting for transfers between devices, placed(): come = lax.ppermute(packed, 'grp', [(0, 1), (1, 0)])  2.01 us
  transfers between devices with their start and end apart: 5, of which 3 were waited for; matrix products, arithmetic and copies ran while one was open for 0% of the time, Pallas kernels for 20%

profile of v2, /device:TPU:0, one launch (start us, length us, event | category | flops | bytes accessed | tf_op | source)
XLA Modules:
  0.0 61.6 jit_solution(11615587426051937824)
XLA Ops:
  0.6 0.0 copy-start
  0.6 0.0 copy-start.1
  0.7 0.0 copy-start.2
  0.7 3.5 %route.1 = (bf16[1024,256]{1,0:T(8,128)(2,1)}, f32[8,128]{1,0:T(8,128)S(1)}) custom-call(s32[1]{0:T(128)} %bitcast.group_ref, s32[32,64]{1,0:T(8,128)} %label_ref.1, bf16[32,64,128]{2,1,0:T(8,128)(2,1)} %heat_in.1, bf16[32,64,128]{2,1,0:T(8,128)(2,1)} %moist_in.1), custom_call_target="tpu_custom_call" | custom-call | flops 1073741824 | bytes 2097152 | tf_op jit(solution)/shard_map/route/pallas_call | solution.py:475
  4.2 7.4 %all-to-all-start = ((bf16[16,64,256]{2,1,0:T(8,128)(2,1)}), bf16[16,64,256]{2,1,0:T(8,128)(2,1)S(1)}, u32[]{:S(2)}, u32[]{:S(2)}) async-start(bf16[16,64,256]{2,1,0:T(8,128)(2,1)} %bitcast.2), calls=%async_computation | async-start | bytes 1048576 | tf_op jit(solution)/shard_map/all_to_all | solution.py:472
  11.6 0.0 copy-done
  11.6 0.0 copy-done.1
  11.6 0.0 copy-done.2
  11.6 0.1 edges.1
  11.7 0.5 collective-permute-start.2
  12.2 4.0 %collective-permute-start.3 = (bf16[21,40,128]{2,1,0:T(8,128)(2,1)S(1)}, bf16[21,40,128]{2,1,0:T(8,128)(2,1)S(1)}, u32[]{:S(2)}, u32[]{:S(2)}) collective-permute-start(bf16[21,40,128]{2,1,0:T(8,128)(2,1)S(1)} %get-tuple-element.46), channel_id=1, source_target_pairs={{1,0},{2,1},{3,2},{4,3},{5,4},{6,5},{7,6},{8,7},{9,8},{10,9},{11,1... | collective-permute-start | bytes 645128 | tf_op jit(solution)/shard_map/ppermute | solution.py:444
  16.2 10.3 %all-to-all-done = bf16[16,64,256]{2,1,0:T(8,128)(2,1)S(1)} async-done(((bf16[16,64,256]{2,1,0:T(8,128)(2,1)}), bf16[16,64,256]{2,1,0:T(8,128)(2,1)S(1)}, u32[]{:S(2)}, u32[]{:S(2)}) %all-to-all-start) | async-done | bytes 524320 | tf_op jit(solution)/shard_map/all_to_all | solution.py:472
  26.6 0.0 copy-start.5
  26.6 0.0 copy-start.6
  26.6 4.8 %front.1.two_ref = bf16[1024,1024]{1,0:T(8,128)(2,1)S(1)} custom-call(bf16[1024,256]{1,0:T(8,128)(2,1)S(1)} %bitcast.9, bf16[1,256,1024]{2,1,0:T(8,128)(2,1)} %first_in.1, bf16[1,1024,1024]{2,1,0:T(8,128)(2,1)} %second_in.1), custom_call_target="tpu_custom_call" | custom-call | flops 2684354560 | bytes 2621440 | tf_op jit(solution)/shard_map/front/pallas_call | solution.py:274
  31.4 0.0 collective-permute-done.2._.left_in
  31.4 0.0 collective-permute-done.3.__.right_in
  31.4 0.0 copy-done.5
  31.4 0.0 copy-done.6
  31.4 0.0 copy-start.3
  31.4 0.0 copy-start.4
  31.4 4.0 %back.1 = (bf16[1024,256]{1,0:T(8,128)(2,1)}, f32[8,128]{1,0:T(8,128)S(1)}) custom-call(bf16[1024,1024]{1,0:T(8,128)(2,1)S(1)} %front.1.two_ref, bf16[1024,1024]{1,0:T(8,128)(2,1)S(1)} %bitcast.11, bf16[1024,256]{1,0:T(8,128)(2,1)S(1)} %bitcast.12, bf16[21,40,128]{2,1,0:T(8,128)(2,1)S(1)} %collective-permute-done.2._.left_in, ...), custom_call_target="tpu_custom_call" | custom-call | flops 2684354560 | bytes 2621440 | tf_op jit(solution)/shard_map/back/pallas_call | solution.py:290
  35.4 5.9 %all-to-all-start.1 = ((bf16[16,64,256]{2,1,0:T(8,128)(2,1)}), bf16[16,64,256]{2,1,0:T(8,128)(2,1)S(1)}, u32[]{:S(2)}, u32[]{:S(2)}) async-start(bf16[16,64,256]{2,1,0:T(8,128)(2,1)} %bitcast.7), calls=%async_computation.1 | async-start | bytes 1048576 | tf_op jit(solution)/shard_map/all_to_all | solution.py:472
  41.3 0.0 copy-done.3
  41.3 1.0 %plan.1 = (f32[128,16]{1,0:T(8,128)S(1)}, f32[8,128]{1,0:T(8,128)S(1)}, s32[1]{0:T(128)}) custom-call(s32[1]{0:T(128)} %bitcast.group_ref, s32[32,64]{1,0:T(8,128)S(1)} %copy-done.3, f32[8,128]{1,0:T(8,128)S(1)} %get-tuple-element.44._), custom_call_target="tpu_custom_call" | custom-call | flops 1048576 | bytes 1048576 | tf_op jit(solution)/shard_map/plan/pallas_call | solution.py:154
  43.0 0.0 copy-done.4
  43.0 5.4 %dynamics.1 = (bf16[32,32,128]{2,1,0:T(8,128)(2,1)}, bf16[32,32,128]{2,1,0:T(8,128)(2,1)}, bf16[32,32,128]{2,1,0:T(8,128)(2,1)}, f32[8,128]{1,0:T(8,128)S(1)}) custom-call(s32[1]{0:T(128)} %bitcast.group_ref, f32[1,128]{1,0:T(1,128)S(1)} %bitcast.10, bf16[32,64,128]{2,1,0:T(8,128)(2,1)S(1)} %copy-done, bf16[32,64,128]{2,1,0:T(8,128)(2,1)S(1)} %copy-done.1, ...), custom_call_target="tpu_custom_call" | custom-call | flops 26214400 | bytes 3145728 | tf_op jit(solution)/shard_map/dynamics/pallas_call | solution.py:398
  48.4 7.4 %all-to-all-done.1 = bf16[16,64,256]{2,1,0:T(8,128)(2,1)S(1)} async-done(((bf16[16,64,256]{2,1,0:T(8,128)(2,1)}), bf16[16,64,256]{2,1,0:T(8,128)(2,1)S(1)}, u32[]{:S(2)}, u32[]{:S(2)}) %all-to-all-start.1) | async-done | bytes 524320 | tf_op jit(solution)/shard_map/all_to_all | solution.py:472
  55.8 5.8 %conditional.1 = ((bf16[32,32,128]{2,1,0:T(8,128)(2,1)}, bf16[32,32,128]{2,1,0:T(8,128)(2,1)})) conditional(s32[]{:T(128)} %bitcast.6, (f32[8,128]{1,0:T(8,128)S(1)}, bf16[1024,256]{1,0:T(8,128)(2,1)S(1)}, f32[8,128]{1,0:T(8,128)S(1)}, f32[128,16]{1,0:T(8,128)S(1)}) %tuple.20, (f32[8,128]{1,0:T(8,128)S(1)}, bf16[1024,256]{1,0:T(8,128)(2,1)S(1)}, ...), branch_computations={%region_0.0_spmd, %region_1.0_spmd} | conditional | flops 1073741824 | bytes 5242928 | solution.py:511
  55.8 0.2 pack.2.packed_ref
  56.0 1.6 %collective-permute-start = (bf16[128,256]{1,0:T(8,128)(2,1)S(1)}, bf16[128,256]{1,0:T(8,128)(2,1)S(1)}, u32[]{:S(2)}, u32[]{:S(2)}) collective-permute-start(bf16[128,256]{1,0:T(8,128)(2,1)S(1)} %pack.2.packed_ref), channel_id=1, source_target_pairs={{0,16},{16,0},{1,17},{17,1},{2,18},{18,2},{3,19},{19,3},{4,20},{20... | collective-permute-start | bytes 196616 | tf_op jit(solution)/shard_map/cond/branch_0_fun/ppermute | solution.py:219
  57.6 0.8 %keep.2.kept_ref = bf16[1024,256]{1,0:T(8,128)(2,1)S(1)} custom-call(f32[128,16]{1,0:T(8,128)S(1)} %get-tuple-element.16.column_ref, bf16[1024,256]{1,0:T(8,128)(2,1)S(1)} %get-tuple-element.17.result_ref, bf16[128,256]{1,0:T(8,128)(2,1)S(1)} %pack.2.packed_ref), custom_call_target="tpu_custom_call" | custom-call | flops 536870912 | bytes 1048576 | tf_op jit(solution)/shard_map/cond/branch_0_fun/keep/pallas_call | solution.py:220
  58.4 2.0 %collective-permute-done.come_ref = bf16[128,256]{1,0:T(8,128)(2,1)S(1)} collective-permute-done((bf16[128,256]{1,0:T(8,128)(2,1)S(1)}, bf16[128,256]{1,0:T(8,128)(2,1)S(1)}, u32[]{:S(2)}, u32[]{:S(2)}) %collective-permute-start) | collective-permute-done | bytes 65568 | tf_op jit(solution)/shard_map/cond/branch_0_fun/ppermute | solution.py:219
  60.4 1.2 %place.2 = (bf16[32,32,128]{2,1,0:T(8,128)(2,1)}, bf16[32,32,128]{2,1,0:T(8,128)(2,1)}) custom-call(f32[128,16]{1,0:T(8,128)S(1)} %get-tuple-element.16.column_ref, bf16[1024,256]{1,0:T(8,128)(2,1)S(1)} %keep.2.kept_ref, bf16[128,256]{1,0:T(8,128)(2,1)S(1)} %collective-permute-done.come_ref), custom_call_target="tpu_custom_call" | custom-call | flops 67108864 | bytes 2097152 | tf_op jit(solution)/shard_map/cond/branch_0_fun/place/pallas_call | solution.py:230
Async XLA Ops:
  0.6 11.0 %copy-start = (bf16[32,64,128]{2,1,0:T(8,128)(2,1)S(1)}, bf16[32,64,128]{2,1,0:T(8,128)(2,1)}, u32[]{:S(2)}) copy-start(bf16[32,64,128]{2,1,0:T(8,128)(2,1)} %e_in.1) | copy-start | bytes 1572868
  0.6 11.0 %copy-start.1 = (bf16[32,64,128]{2,1,0:T(8,128)(2,1)S(1)}, bf16[32,64,128]{2,1,0:T(8,128)(2,1)}, u32[]{:S(2)}) copy-start(bf16[32,64,128]{2,1,0:T(8,128)(2,1)} %n_in.1) | copy-start | bytes 1572868
  0.7 11.0 %copy-start.2 = (bf16[32,64,128]{2,1,0:T(8,128)(2,1)S(1)}, bf16[32,64,128]{2,1,0:T(8,128)(2,1)}, u32[]{:S(2)}) copy-start(bf16[32,64,128]{2,1,0:T(8,128)(2,1)} %p_in.1) | copy-start | bytes 1572868
  4.2 22.3 %all-to-all-start = ((bf16[16,64,256]{2,1,0:T(8,128)(2,1)}), bf16[16,64,256]{2,1,0:T(8,128)(2,1)S(1)}, u32[]{:S(2)}, u32[]{:S(2)}) async-start(bf16[16,64,256]{2,1,0:T(8,128)(2,1)} %bitcast.2), calls=%async_computation | async-start | bytes 1048576 | tf_op jit(solution)/shard_map/all_to_all | solution.py:472
  11.7 19.6 %collective-permute-start.2 = (bf16[21,40,128]{2,1,0:T(8,128)(2,1)S(1)}, bf16[21,40,128]{2,1,0:T(8,128)(2,1)S(1)}, u32[]{:S(2)}, u32[]{:S(2)}) collective-permute-start(bf16[21,40,128]{2,1,0:T(8,128)(2,1)S(1)} %get-tuple-element.45), channel_id=1, source_target_pairs={{0,1},{1,2},{2,3},{3,4},{4,5},{5,6},{6,7},{7,8},{8,9},{9,10},{10,1... | collective-permute-start | bytes 645128 | tf_op jit(solution)/shard_map/ppermute | solution.py:443
  12.2 19.2 %collective-permute-start.3 = (bf16[21,40,128]{2,1,0:T(8,128)(2,1)S(1)}, bf16[21,40,128]{2,1,0:T(8,128)(2,1)S(1)}, u32[]{:S(2)}, u32[]{:S(2)}) collective-permute-start(bf16[21,40,128]{2,1,0:T(8,128)(2,1)S(1)} %get-tuple-element.46), channel_id=1, source_target_pairs={{1,0},{2,1},{3,2},{4,3},{5,4},{6,5},{7,6},{8,7},{9,8},{10,9},{11,1... | collective-permute-start | bytes 645128 | tf_op jit(solution)/shard_map/ppermute | solution.py:444
  26.6 4.8 %copy-start.5 = (bf16[1,1024,1024]{2,1,0:T(8,128)(2,1)S(1)}, bf16[1,1024,1024]{2,1,0:T(8,128)(2,1)}, u32[]{:S(2)}) copy-start(bf16[1,1024,1024]{2,1,0:T(8,128)(2,1)} %param.22) | copy-start | bytes 6291460
  26.6 4.8 %copy-start.6 = (bf16[1,1024,256]{2,1,0:T(8,128)(2,1)S(1)}, bf16[1,1024,256]{2,1,0:T(8,128)(2,1)}, u32[]{:S(2)}) copy-start(bf16[1,1024,256]{2,1,0:T(8,128)(2,1)} %param.23) | copy-start | bytes 1572868
  31.4 9.9 %copy-start.3 = (s32[32,64]{1,0:T(8,128)S(1)}, s32[32,64]{1,0:T(8,128)}, u32[]{:S(2)}) copy-start(s32[32,64]{1,0:T(8,128)} %label_ref.1) | copy-start | bytes 24580
  31.4 11.6 %copy-start.4 = (f32[128]{0:T(128)S(1)}, f32[128]{0:T(128)}, u32[]{:S(2)}) copy-start(f32[128]{0:T(128)} %param.19) | copy-start | bytes 1540
  35.4 20.4 %all-to-all-start.1 = ((bf16[16,64,256]{2,1,0:T(8,128)(2,1)}), bf16[16,64,256]{2,1,0:T(8,128)(2,1)S(1)}, u32[]{:S(2)}, u32[]{:S(2)}) async-start(bf16[16,64,256]{2,1,0:T(8,128)(2,1)} %bitcast.7), calls=%async_computation.1 | async-start | bytes 1048576 | tf_op jit(solution)/shard_map/all_to_all | solution.py:472
  56.0 4.3 %collective-permute-start = (bf16[128,256]{1,0:T(8,128)(2,1)S(1)}, bf16[128,256]{1,0:T(8,128)(2,1)S(1)}, u32[]{:S(2)}, u32[]{:S(2)}) collective-permute-start(bf16[128,256]{1,0:T(8,128)(2,1)S(1)} %pack.2.packed_ref), channel_id=1, source_target_pairs={{0,16},{16,0},{1,17},{17,1},{2,18},{18,2},{3,19},{19,3},{4,20},{20... | collective-permute-start | bytes 196616 | tf_op jit(solution)/shard_map/cond/branch_0_fun/ppermute | solution.py:219

commit v3 on v2

--- a/solution.py
+++ b/solution.py
@@ -7,7 +7,8 @@
 from jax.sharding import PartitionSpec as P
 
 SUB = 4
-ROOM = 128
+BATCHES = 2
+ROOM = 80
 LANES = 128
 MIB = 1 << 20
 bf16, f32, i32 = jnp.bfloat16, jnp.float32, jnp.int32
@@ -50,20 +51,17 @@
     first = lax.broadcasted_iota(i32, (LANES, LANES), 0)
     second = lax.broadcasted_iota(i32, (LANES, LANES), 1)
     earlier = jnp.where(first < second, 1.0, 0.0).astype(bf16)
-    within = jnp.dot(flat, earlier, preferred_element_type=f32).reshape(shape)
-    totals = jnp.dot(
-        flat, jnp.ones((LANES, LANES), bf16), preferred_element_type=f32
-    ).reshape(shape)
-    before = jnp.zeros((regimes, 1, LANES), f32)
-    rank = jnp.zeros((rows, LANES), f32)
-    row_ranks = []
-    for m in range(rows):
-        row_ranks.append(
-            jnp.sum(member[:, m : m + 1] * (within[:, m : m + 1] + before), axis=0)
-        )
-        before = before + totals[:, m : m + 1]
-    rank = jnp.concatenate(row_ranks, axis=0)
-    return rank, member, before
+    totals = jnp.dot(flat, jnp.ones((LANES, LANES), bf16), preferred_element_type=f32)
+    within = jnp.dot(flat, earlier, preferred_element_type=f32)
+    totals = totals.reshape(shape)
+    row = lax.broadcasted_iota(i32, (1, rows, LANES), 1)
+    before, step = totals, 1
+    while step < rows:
+        before = before + jnp.where(row >= step, pltpu.roll(before, step, 1), 0.0)
+        step *= 2
+    count = before[:, rows - 1 :]
+    rank = jnp.sum(member * (within.reshape(shape) + (before - totals)), axis=0)
+    return rank, member, count
 
 
 def route_kernel(
@@ -104,11 +102,13 @@
     soundings = jnp.concatenate(columns, axis=0)
     total = out_ref.shape[0]
     tile = min(256, total)
+    slot = lax.broadcasted_iota(i32, (tile, LANES), 0).astype(f32).astype(bf16)
+    yes, no = jnp.ones((), bf16), jnp.zeros((), bf16)
     for start in range(0, total, tile):
-        slot = (lax.broadcasted_iota(i32, (tile, LANES), 0) + start).astype(f32)
+        near = target - start
+        near = jnp.where((near >= 0) & (near < tile), near, -1.0).astype(bf16)
         picks = jnp.concatenate(
-            [jnp.where(slot == target[m : m + 1], 1.0, 0.0).astype(bf16) for m in range(2 * rows)],
-            axis=1,
+            [jnp.where(slot == near[m : m + 1], yes, no) for m in range(2 * rows)], axis=1
         )
         out_ref[start : start + tile] = jnp.dot(
             picks, soundings, preferred_element_type=f32
@@ -251,37 +251,80 @@
         target[:, at] = silu(sums).astype(bf16)
 
 
-def front_kernel(x_ref, first_in, second_in, out_ref, one_ref, first_ref, second_ref, sem):
-    first = pltpu.make_async_copy(first_in.at[0], first_ref, sem.at[0])
-    second = pltpu.make_async_copy(second_in.at[0], second_ref, sem.at[1])
-    first.start()
-    second.start()
-    first.wait()
+def fetch_kernel(first_in, second_in, _, first_ref, second_ref, sem):
+    copies = [
+        pltpu.make_async_copy(first_in.at[0], first_ref, sem.at[0]),
+        pltpu.make_async_copy(
+            second_in.at[0, :, : second_ref.shape[1]], second_ref, sem.at[1]
+        ),
+    ]
+    for copy in copies:
+        copy.start()
+    for copy in copies:
+        copy.wait()
+
+
+def fetched(first, second, after):
+    return pl.pallas_call(
+        fetch_kernel,
+        out_shape=(
+            pltpu.VMEM(first.shape[1:], bf16),
+            pltpu.VMEM((second.shape[1], second.shape[2] // 2), bf16),
+        ),
+        in_specs=[HBM, HBM, VMEM],
+        out_specs=(VMEM, VMEM),
+        scratch_shapes=[pltpu.SemaphoreType.DMA((2,))],
+        compiler_params=params(6),
+        cost_estimate=cost(0, 2 * first.size + second.size),
+        name="fetch",
+    )(*in_hbm(first, second), after)
+
+
+def front_kernel(x_ref, first_ref, left_ref, second_in, out_ref, one_ref, right_ref, sem):
+    near = left_ref.shape[1]
+    copy = pltpu.make_async_copy(second_in.at[0, :, near:], right_ref, sem.at[0])
+    copy.start()
     layer(x_ref, first_ref, one_ref)
-    second.wait()
-    layer(one_ref, second_ref, out_ref)
-
-
-def back_kernel(two_ref, third_ref, last_ref, _, __, out_ref, token_ref, three_ref):
+    layer(one_ref, left_ref, out_ref.at[:, :near])
+    copy.wait()
+    layer(one_ref, right_ref, out_ref.at[:, near:])
+
+
+def back_kernel(
+    two_ref, third_ref, last_ref, _, __, out_hbm, token_ref, three_ref, out_ref, sem
+):
     token_ref[...] = jnp.zeros_like(token_ref)
-    layer(two_ref, third_ref, three_ref)
-    out_ref[...] = jnp.dot(three_ref[...], last_ref[...], preferred_element_type=f32).astype(bf16)
-
-
-def front(x, first, second):
-    rows, hidden = x.shape[0], first.shape[2]
+    piece = out_ref.shape[0] // BATCHES
+    copies = []
+    for i in range(BATCHES):
+        at = slice(i * piece, (i + 1) * piece)
+        layer(two_ref.at[at], third_ref, three_ref.at[at])
+        out_ref[at] = jnp.dot(
+            three_ref[at], last_ref[...], preferred_element_type=f32
+        ).astype(bf16)
+        copies.append(pltpu.make_async_copy(out_ref.at[at], out_hbm.at[at], sem.at[i]))
+        copies[-1].start()
+    for copy in copies:
+        copy.wait()
+
+
+def front(x, first, left, second):
+    rows, hidden = x.shape[0], first.shape[1]
     size = first.size + second.size
+    first, left = [pltpu.with_memory_space_constraint(w, pltpu.VMEM) for w in (first, left)]
     return pl.pallas_call(
         front_kernel,
         out_shape=jax.ShapeDtypeStruct((rows, hidden), bf16),
-        in_specs=[VMEM] + [HBM] * 2,
-        scratch_shapes=[pltpu.VMEM((rows, hidden), bf16)]
-        + [pltpu.VMEM(w.shape[1:], bf16) for w in (first, second)]
-        + [pltpu.SemaphoreType.DMA((2,))],
+        in_specs=[VMEM] * 3 + [HBM],
+        scratch_shapes=[
+            pltpu.VMEM((rows, hidden), bf16),
+            pltpu.VMEM((second.shape[1], second.shape[2] - left.shape[1]), bf16),
+            pltpu.SemaphoreType.DMA((1,)),
+        ],
         compiler_params=params(14),
         cost_estimate=cost(2 * rows * size, 2 * size),
         name="front",
-    )(x, *in_hbm(first, second))
+    )(x, first, left, *in_hbm(second))
 
 
 def back(two, third, last, *after):
@@ -291,7 +334,12 @@
         back_kernel,
         out_shape=(jax.ShapeDtypeStruct((rows, last.shape[1]), bf16), TOKEN),
         in_specs=[VMEM] * 3 + [ANY] * len(after),
-        scratch_shapes=[pltpu.VMEM((rows, hidden), bf16)],
+        out_specs=(HBM, VMEM),
+        scratch_shapes=[
+            pltpu.VMEM((rows, hidden), bf16),
+            pltpu.VMEM((rows, last.shape[1]), bf16),
+            pltpu.SemaphoreType.DMA((BATCHES,)),
+        ],
         compiler_params=params(14),
         cost_estimate=cost(2 * rows * size, 2 * size),
         name="back",
@@ -299,9 +347,15 @@
 
 
 def dynamics_kernel(
-    group_ref, rate_ref, e_in, n_in, p_in, left_in, right_in, _, e_out, n_out, p_out, token_ref,
-    e_ref, n_ref, p_ref, left_ref, right_ref, sem,
+    group_ref, rate_ref, e_hbm, n_hbm, p_hbm, left_in, right_in, _, e_out, n_out, p_out, token_ref,
+    e_ref, n_ref, p_ref, e_in, n_in, p_in, left_ref, right_ref, sem,
 ):
+    inputs = [
+        pltpu.make_async_copy(source, target, sem.at[2 + i])
+        for i, (source, target) in enumerate(((e_hbm, e_in), (n_hbm, n_in), (p_hbm, p_in)))
+    ]
+    for copy in inputs:
+        copy.start()
     sides = [
         pltpu.make_async_copy(left_in, left_ref, sem.at[0]),
         pltpu.make_async_copy(right_in, right_ref, sem.at[1]),
@@ -333,6 +387,9 @@
         (n_in, n_out, n_ref, 8, reach - 2),
     )
 
+    for copy in inputs:
+        copy.wait()
+
     def load(i, _):
         for source, _, ref, off, width in fields:
             row = source[i].astype(f32)
@@ -398,33 +455,47 @@
     return pl.pallas_call(
         dynamics_kernel,
         out_shape=(out,) * 3 + (TOKEN,),
-        in_specs=[SMEM] + [VMEM] * 4 + [ANY] * 2 + [VMEM],
+        in_specs=[SMEM, VMEM] + [HBM] * 3 + [ANY] * 2 + [VMEM],
         scratch_shapes=[
             pltpu.VMEM((deep + 2 * (reach - 1), span, levels), f32),
             pltpu.VMEM((deep + 2 * (reach - 2), span + 16, levels), f32),
             pltpu.VMEM((deep + 2 * reach, span + 16, levels), f32),
+            *[pltpu.VMEM(e.shape, bf16)] * 3,
             pltpu.VMEM(left.shape, bf16),
             pltpu.VMEM(right.shape, bf16),
-            pltpu.SemaphoreType.DMA((2,)),
+            pltpu.SemaphoreType.DMA((5,)),
         ],
         compiler_params=params(12),
         cost_estimate=cost(cells * 200, cells * 24),
         name="dynamics",
-    )(group, rate, e, n, p, left, right, after)
-
-
-def edges_kernel(group_ref, e_ref, n_ref, p_ref, _, tail_ref, head_ref):
-    deep, wide = e_ref.shape[:2]
+    )(group, rate, *in_hbm(e, n, p), left, right, after)
+
+
+def edges_kernel(group_ref, e_in, n_in, p_in, _, tail_ref, head_ref, last_ref, first_ref, sem):
+    deep, wide = e_in.shape[:2]
     span = tail_ref.shape[1]
     mine = group_ref[0]
     reach = 2 * SUB
+    copies = []
     at = 0
-    for ref, width in ((p_ref, reach), (e_ref, reach - 1), (n_ref, reach - 2)):
-        for i in range(width):
-            for out, row in ((tail_ref, deep - width + i), (head_ref, i)):
-                whole = ref[row].astype(f32)
-                out[at + i] = jnp.where(mine == 0, whole[:span], whole[wide - span :]).astype(bf16)
+    for source, width in ((p_in, reach), (e_in, reach - 1), (n_in, reach - 2)):
+        for target, start in ((last_ref, deep - width), (first_ref, 0)):
+            copies.append(
+                pltpu.make_async_copy(
+                    source.at[start : start + width],
+                    target.at[at : at + width],
+                    sem.at[len(copies)],
+                )
+            )
         at += width
+    for copy in copies:
+        copy.start()
+    for copy in copies:
+        copy.wait()
+    for source, out in ((last_ref, tail_ref), (first_ref, head_ref)):
+        for i in range(at):
+            whole = source[i].astype(f32)
+            out[i] = jnp.where(mine == 0, whole[:span], whole[wide - span :]).astype(bf16)
 
 
 def halos(group, e, n, p, after):
@@ -435,11 +506,13 @@
     tail, head = pl.pallas_call(
         edges_kernel,
         out_shape=(out, out),
-        in_specs=[SMEM] + [VMEM] * 4,
-        compiler_params=params(12),
+        in_specs=[SMEM] + [HBM] * 3 + [VMEM],
+        scratch_shapes=[pltpu.VMEM((3 * reach - 3, wide, levels), bf16)] * 2
+        + [pltpu.SemaphoreType.DMA((6,))],
+        compiler_params=params(6),
         cost_estimate=cost(MIB, 2 * MIB),
         name="edges",
-    )(group, e, n, p, after)
+    )(group, *in_hbm(e, n, p), after)
     left = lax.ppermute(tail, "blk", [(i, (i + 1) % count) for i in range(count)])
     right = lax.ppermute(head, "blk", [((i + 1) % count, i) for i in range(count)])
     return left, right
@@ -494,7 +567,11 @@
         group, zonal_velocity_field, meridional_velocity_field, barometric_disturbance, routed
     )
     column_plan, pack_plan, crowded = plan(regimes, part, rows, group, flow_category_label, routed)
-    two = front(arrived, initial_dense_matrix, middle_dense_matrix)
+    two = front(
+        arrived,
+        *fetched(initial_dense_matrix, middle_dense_matrix, routed),
+        middle_dense_matrix,
+    )
     result, worked = back(two, closing_dense_matrix[0], final_readout_matrix[0], left, right)
     returned = swapped(result)
     east, north, pressure, moved = dynamics(

time: 61.9 us -> 60.3 us (0.974)
  waiting for transfers between devices: 19.7 us -> 16.6 us
  Pallas kernels: 21 us -> 22.4 us
    all_to_all x2, waiting for transfers between devices: 17.7 us -> 14.9 us  [swapped(): one = lax.all_to_all(one, 'blk', split_axis=0, concat_axis=0, tiled=True)]
    pallas_call x1 -> x2, Pallas kernels: 0.1 us -> 2.73 us  [the longest x1 1.4 us: fetched(): pl.pallas_call(fetch_kernel, out_shape=(pltpu.VMEM(first.shape[1:], bf16)...]
    pallas_call x1, Pallas kernels: 4.8 us -> 3.56 us  [front(): pl.pallas_call(front_kernel, out_shape=jax.ShapeDtypeStruct((rows, hidden...]
  transfers between devices with their start and end apart: 5 -> 5, of which waited for: 3 -> 3; matrix products, arithmetic and copies ran while one was open for 0% -> 0% of each run, Pallas kernels for 20% -> 23%
where the time goes in v3:
time: 60.3 us; the launch traced here: 59.9 us
  Pallas kernels  22.4 us (37%)
  starting transfers between devices  19.4 us (32%)
  waiting for transfers between devices  16.6 us (28%)
  between operations  1.42 us (2%)
    all_to_all x2, waiting for transfers between devices, swapped(): one = lax.all_to_all(one, 'blk', split_axis=0, concat_axis=0, tiled=True)  14.9 us
    all_to_all x2, starting transfers between devices, swapped(): one = lax.all_to_all(one, 'blk', split_axis=0, concat_axis=0, tiled=True)  13.3 us
    pallas_call x1, Pallas kernels, dynamics(): pl.pallas_call(dynamics_kernel, out_shape=(out,) * 3 + (TOKEN,), in_specs...  5.68 us
    ppermute x1, starting transfers between devices, halos(): lax.ppermute(head, 'blk', [((i + 1) % count, i) for i in range(count)])  4.04 us
    pallas_call x1, Pallas kernels, back(): pl.pallas_call(back_kernel, out_shape=(jax.ShapeDtypeStruct((rows, last.s...  3.92 us
    pallas_call x1, Pallas kernels, front(): pl.pallas_call(front_kernel, out_shape=jax.ShapeDtypeStruct((rows, hidden...  3.56 us
    pallas_call x1, Pallas kernels, local(): pl.pallas_call(functools.partial(route_kernel, regimes, part), out_shape=...  3.43 us
    ppermute x1, waiting for transfers between devices, placed(): come = lax.ppermute(packed, 'grp', [(0, 1), (1, 0)])  1.73 us
  transfers between devices with their start and end apart: 5, of which 3 were waited for; matrix products, arithmetic and copies ran while one was open for 0% of the time, Pallas kernels for 23%

profile of v3, /device:TPU:0, one launch (start us, length us, event | category | flops | bytes accessed | tf_op | source)
XLA Modules:
  0.0 59.9 jit_solution(16224278924579425342)
XLA Ops:
  0.6 3.4 %route.1 = (bf16[1024,256]{1,0:T(8,128)(2,1)}, f32[8,128]{1,0:T(8,128)S(1)}) custom-call(s32[1]{0:T(128)} %bitcast.group_ref, s32[32,64]{1,0:T(8,128)} %label_ref.1, bf16[32,64,128]{2,1,0:T(8,128)(2,1)} %heat_in.1, bf16[32,64,128]{2,1,0:T(8,128)(2,1)} %moist_in.1), custom_call_target="tpu_custom_call" | custom-call | flops 1073741824 | bytes 2097152 | tf_op jit(solution)/shard_map/route/pallas_call | solution.py:548
  4.1 7.4 %all-to-all-start = ((bf16[16,64,256]{2,1,0:T(8,128)(2,1)}), bf16[16,64,256]{2,1,0:T(8,128)(2,1)S(1)}, u32[]{:S(2)}, u32[]{:S(2)}) async-start(bf16[16,64,256]{2,1,0:T(8,128)(2,1)} %bitcast.2), calls=%async_computation | async-start | bytes 1048576 | tf_op jit(solution)/shard_map/all_to_all | solution.py:545
  11.5 1.3 %edges.1 = (bf16[21,40,128]{2,1,0:T(8,128)(2,1)S(1)}, bf16[21,40,128]{2,1,0:T(8,128)(2,1)S(1)}) custom-call(s32[1]{0:T(128)} %bitcast.group_ref, bf16[32,64,128]{2,1,0:T(8,128)(2,1)} %e_hbm.1, bf16[32,64,128]{2,1,0:T(8,128)(2,1)} %n_hbm.1, bf16[32,64,128]{2,1,0:T(8,128)(2,1)} %p_hbm.1, f32[8,128]{1,0:T(8,128)S(1)} %get-tuple-element.46._), custom_call_target="tpu_custom_call" | custom-call | flops 1048576 | bytes 2097152 | tf_op jit(solution)/shard_map/edges/pallas_call | solution.py:506
  12.8 0.5 collective-permute-start.2
  13.3 4.0 %collective-permute-start.3 = (bf16[21,40,128]{2,1,0:T(8,128)(2,1)S(1)}, bf16[21,40,128]{2,1,0:T(8,128)(2,1)S(1)}, u32[]{:S(2)}, u32[]{:S(2)}) collective-permute-start(bf16[21,40,128]{2,1,0:T(8,128)(2,1)S(1)} %get-tuple-element.48), channel_id=1, source_target_pairs={{1,0},{2,1},{3,2},{4,3},{5,4},{6,5},{7,6},{8,7},{9,8},{10,9},{11,1... | collective-permute-start | bytes 645128 | tf_op jit(solution)/shard_map/ppermute | solution.py:517
  17.3 1.4 %fetch.1 = (bf16[256,1024]{1,0:T(8,128)(2,1)S(1)}, bf16[1024,512]{1,0:T(8,128)(2,1)S(1)}) custom-call(bf16[1,256,1024]{2,1,0:T(8,128)(2,1)} %first_in.1, bf16[1,1024,1024]{2,1,0:T(8,128)(2,1)} %second_in.3, f32[8,128]{1,0:T(8,128)S(1)} %get-tuple-element.46._), custom_call_target="tpu_custom_call" | custom-call | bytes 1572864 | tf_op jit(solution)/shard_map/fetch/pallas_call | solution.py:268
  18.7 7.7 %all-to-all-done = bf16[16,64,256]{2,1,0:T(8,128)(2,1)S(1)} async-done(((bf16[16,64,256]{2,1,0:T(8,128)(2,1)}), bf16[16,64,256]{2,1,0:T(8,128)(2,1)S(1)}, u32[]{:S(2)}, u32[]{:S(2)}) %all-to-all-start) | async-done | bytes 524320 | tf_op jit(solution)/shard_map/all_to_all | solution.py:545
  26.4 0.0 copy-start.2
  26.4 0.0 copy-start.3
  26.4 3.6 %front.1.two_ref = bf16[1024,1024]{1,0:T(8,128)(2,1)S(1)} custom-call(bf16[1024,256]{1,0:T(8,128)(2,1)S(1)} %bitcast.9, bf16[256,1024]{1,0:T(8,128)(2,1)S(1)} %get-tuple-element.50.first_ref, bf16[1024,512]{1,0:T(8,128)(2,1)S(1)} %get-tuple-element.51.left_ref, bf16[1,1024,1024]{2,1,0:T(8,128)(2,1)} %second_in.3), custom_call_target="tpu_custom_call" | custom-call | flops 2684354560 | bytes 2621440 | tf_op jit(solution)/shard_map/front/pallas_call | solution.py:315
  30.0 0.0 collective-permute-done.2._.left_in
  30.0 0.0 collective-permute-done.3.__.right_in
  30.0 0.0 copy-done.2
  30.0 0.0 copy-done.3
  30.0 0.0 copy-start
  30.0 0.0 copy-start.1
  30.1 3.9 %back.1 = (bf16[1024,256]{1,0:T(8,128)(2,1)}, f32[8,128]{1,0:T(8,128)S(1)}) custom-call(bf16[1024,1024]{1,0:T(8,128)(2,1)S(1)} %front.1.two_ref, bf16[1024,1024]{1,0:T(8,128)(2,1)S(1)} %bitcast.11, bf16[1024,256]{1,0:T(8,128)(2,1)S(1)} %bitcast.12, bf16[21,40,128]{2,1,0:T(8,128)(2,1)S(1)} %collective-permute-done.2._.left_in, ...), custom_call_target="tpu_custom_call" | custom-call | flops 2684354560 | bytes 2621440 | tf_op jit(solution)/shard_map/back/pallas_call | solution.py:333
  34.0 5.9 %all-to-all-start.1 = ((bf16[16,64,256]{2,1,0:T(8,128)(2,1)}), bf16[16,64,256]{2,1,0:T(8,128)(2,1)S(1)}, u32[]{:S(2)}, u32[]{:S(2)}) async-start(bf16[16,64,256]{2,1,0:T(8,128)(2,1)} %bitcast.7), calls=%async_computation.1 | async-start | bytes 1048576 | tf_op jit(solution)/shard_map/all_to_all | solution.py:545
  39.9 0.0 copy-done
  39.9 0.9 %plan.1 = (f32[128,16]{1,0:T(8,128)S(1)}, f32[8,128]{1,0:T(8,128)S(1)}, s32[1]{0:T(128)}) custom-call(s32[1]{0:T(128)} %bitcast.group_ref, s32[32,64]{1,0:T(8,128)S(1)} %copy-done, f32[8,128]{1,0:T(8,128)S(1)} %get-tuple-element.46._), custom_call_target="tpu_custom_call" | custom-call | flops 1048576 | bytes 1048576 | tf_op jit(solution)/shard_map/plan/pallas_call | solution.py:154
  41.5 0.0 copy-done.1
  41.5 5.7 %dynamics.1 = (bf16[32,32,128]{2,1,0:T(8,128)(2,1)}, bf16[32,32,128]{2,1,0:T(8,128)(2,1)}, bf16[32,32,128]{2,1,0:T(8,128)(2,1)}, f32[8,128]{1,0:T(8,128)S(1)}) custom-call(s32[1]{0:T(128)} %bitcast.group_ref, f32[1,128]{1,0:T(1,128)S(1)} %bitcast.10, bf16[32,64,128]{2,1,0:T(8,128)(2,1)} %e_hbm.1, bf16[32,64,128]{2,1,0:T(8,128)(2,1)} %n_hbm.1, ...), custom_call_target="tpu_custom_call" | custom-call | flops 26214400 | bytes 3145728 | tf_op jit(solution)/shard_map/dynamics/pallas_call | solution.py:455
  47.2 7.2 %all-to-all-done.1 = bf16[16,64,256]{2,1,0:T(8,128)(2,1)S(1)} async-done(((bf16[16,64,256]{2,1,0:T(8,128)(2,1)}), bf16[16,64,256]{2,1,0:T(8,128)(2,1)S(1)}, u32[]{:S(2)}, u32[]{:S(2)}) %all-to-all-start.1) | async-done | bytes 524320 | tf_op jit(solution)/shard_map/all_to_all | solution.py:545
  54.4 5.5 %conditional.1 = ((bf16[32,32,128]{2,1,0:T(8,128)(2,1)}, bf16[32,32,128]{2,1,0:T(8,128)(2,1)})) conditional(s32[]{:T(128)} %bitcast.6, (f32[8,128]{1,0:T(8,128)S(1)}, bf16[1024,256]{1,0:T(8,128)(2,1)S(1)}, f32[8,128]{1,0:T(8,128)S(1)}, f32[128,16]{1,0:T(8,128)S(1)}) %tuple.20, (f32[8,128]{1,0:T(8,128)S(1)}, bf16[1024,256]{1,0:T(8,128)(2,1)S(1)}, ...), branch_computations={%region_0.0_spmd, %region_1.0_spmd} | conditional | flops 1073741824 | bytes 5242928 | solution.py:588
  54.4 0.2 pack.2.packed_ref
  54.6 1.6 %collective-permute-start = (bf16[80,256]{1,0:T(8,128)(2,1)S(1)}, bf16[80,256]{1,0:T(8,128)(2,1)S(1)}, u32[]{:S(2)}, u32[]{:S(2)}) collective-permute-start(bf16[80,256]{1,0:T(8,128)(2,1)S(1)} %pack.2.packed_ref), channel_id=1, source_target_pairs={{0,16},{16,0},{1,17},{17,1},{2,18},{18,2},{3,19},{19,3},{4,20},{20... | collective-permute-start | bytes 122888 | tf_op jit(solution)/shard_map/cond/branch_0_fun/ppermute | solution.py:219
  56.2 0.8 %keep.2.kept_ref = bf16[1024,256]{1,0:T(8,128)(2,1)S(1)} custom-call(f32[128,16]{1,0:T(8,128)S(1)} %get-tuple-element.16.column_ref, bf16[1024,256]{1,0:T(8,128)(2,1)S(1)} %get-tuple-element.17.result_ref, bf16[80,256]{1,0:T(8,128)(2,1)S(1)} %pack.2.packed_ref), custom_call_target="tpu_custom_call" | custom-call | flops 536870912 | bytes 1048576 | tf_op jit(solution)/shard_map/cond/branch_0_fun/keep/pallas_call | solution.py:220
  56.9 1.7 %collective-permute-done.come_ref = bf16[80,256]{1,0:T(8,128)(2,1)S(1)} collective-permute-done((bf16[80,256]{1,0:T(8,128)(2,1)S(1)}, bf16[80,256]{1,0:T(8,128)(2,1)S(1)}, u32[]{:S(2)}, u32[]{:S(2)}) %collective-permute-start) | collective-permute-done | bytes 40992 | tf_op jit(solution)/shard_map/cond/branch_0_fun/ppermute | solution.py:219
  58.7 1.2 %place.2 = (bf16[32,32,128]{2,1,0:T(8,128)(2,1)}, bf16[32,32,128]{2,1,0:T(8,128)(2,1)}) custom-call(f32[128,16]{1,0:T(8,128)S(1)} %get-tuple-element.16.column_ref, bf16[1024,256]{1,0:T(8,128)(2,1)S(1)} %keep.2.kept_ref, bf16[80,256]{1,0:T(8,128)(2,1)S(1)} %collective-permute-done.come_ref), custom_call_target="tpu_custom_call" | custom-call | flops 41943040 | bytes 2097152 | tf_op jit(solution)/shard_map/cond/branch_0_fun/place/pallas_call | solution.py:230
Async XLA Ops:
  4.1 22.3 %all-to-all-start = ((bf16[16,64,256]{2,1,0:T(8,128)(2,1)}), bf16[16,64,256]{2,1,0:T(8,128)(2,1)S(1)}, u32[]{:S(2)}, u32[]{:S(2)}) async-start(bf16[16,64,256]{2,1,0:T(8,128)(2,1)} %bitcast.2), calls=%async_computation | async-start | bytes 1048576 | tf_op jit(solution)/shard_map/all_to_all | solution.py:545
  12.8 17.2 %collective-permute-start.2 = (bf16[21,40,128]{2,1,0:T(8,128)(2,1)S(1)}, bf16[21,40,128]{2,1,0:T(8,128)(2,1)S(1)}, u32[]{:S(2)}, u32[]{:S(2)}) collective-permute-start(bf16[21,40,128]{2,1,0:T(8,128)(2,1)S(1)} %get-tuple-element.47), channel_id=1, source_target_pairs={{0,1},{1,2},{2,3},{3,4},{4,5},{5,6},{6,7},{7,8},{8,9},{9,10},{10,1... | collective-permute-start | bytes 645128 | tf_op jit(solution)/shard_map/ppermute | solution.py:516
  13.3 16.7 %collective-permute-start.3 = (bf16[21,40,128]{2,1,0:T(8,128)(2,1)S(1)}, bf16[21,40,128]{2,1,0:T(8,128)(2,1)S(1)}, u32[]{:S(2)}, u32[]{:S(2)}) collective-permute-start(bf16[21,40,128]{2,1,0:T(8,128)(2,1)S(1)} %get-tuple-element.48), channel_id=1, source_target_pairs={{1,0},{2,1},{3,2},{4,3},{5,4},{6,5},{7,6},{8,7},{9,8},{10,9},{11,1... | collective-permute-start | bytes 645128 | tf_op jit(solution)/shard_map/ppermute | solution.py:517
  26.4 3.6 %copy-start.2 = (bf16[1,1024,1024]{2,1,0:T(8,128)(2,1)S(1)}, bf16[1,1024,1024]{2,1,0:T(8,128)(2,1)}, u32[]{:S(2)}) copy-start(bf16[1,1024,1024]{2,1,0:T(8,128)(2,1)} %param.22) | copy-start | bytes 6291460
  26.4 3.6 %copy-start.3 = (bf16[1,1024,256]{2,1,0:T(8,128)(2,1)S(1)}, bf16[1,1024,256]{2,1,0:T(8,128)(2,1)}, u32[]{:S(2)}) copy-start(bf16[1,1024,256]{2,1,0:T(8,128)(2,1)} %param.23) | copy-start | bytes 1572868
  30.0 9.9 %copy-start = (s32[32,64]{1,0:T(8,128)S(1)}, s32[32,64]{1,0:T(8,128)}, u32[]{:S(2)}) copy-start(s32[32,64]{1,0:T(8,128)} %label_ref.1) | copy-start | bytes 24580
  30.0 11.5 %copy-start.1 = (f32[128]{0:T(128)S(1)}, f32[128]{0:T(128)}, u32[]{:S(2)}) copy-start(f32[128]{0:T(128)} %param.19) | copy-start | bytes 1540
  34.0 20.4 %all-to-all-start.1 = ((bf16[16,64,256]{2,1,0:T(8,128)(2,1)}), bf16[16,64,256]{2,1,0:T(8,128)(2,1)S(1)}, u32[]{:S(2)}, u32[]{:S(2)}) async-start(bf16[16,64,256]{2,1,0:T(8,128)(2,1)} %bitcast.7), calls=%async_computation.1 | async-start | bytes 1048576 | tf_op jit(solution)/shard_map/all_to_all | solution.py:545
  54.6 4.1 %collective-permute-start = (bf16[80,256]{1,0:T(8,128)(2,1)S(1)}, bf16[80,256]{1,0:T(8,128)(2,1)S(1)}, u32[]{:S(2)}, u32[]{:S(2)}) collective-permute-start(bf16[80,256]{1,0:T(8,128)(2,1)S(1)} %pack.2.packed_ref), channel_id=1, source_target_pairs={{0,16},{16,0},{1,17},{17,1},{2,18},{18,2},{3,19},{19,3},{4,20},{20... | collective-permute-start | bytes 122888 | tf_op jit(solution)/shard_map/cond/branch_0_fun/ppermute | solution.py:219

commit v4 on v3

--- a/solution.py
+++ b/solution.py
@@ -33,11 +33,15 @@
     return pl.CostEstimate(flops=flops, bytes_accessed=moved, transcendentals=0)
 
 
-def folded(labels, start, half):
-    rows = labels.shape[0] * half // LANES
-    side = labels[:, start : start + half]
+def folded(label_ref, start, half):
+    pieces = LANES // half
+    rows = label_ref.shape[0] // pieces
     return jnp.concatenate(
-        [side[t * rows : (t + 1) * rows] for t in range(LANES // half)], axis=1
+        [
+            label_ref[pl.ds(t, rows, stride=pieces), :][:, start : start + half]
+            for t in range(pieces)
+        ],
+        axis=1,
     )
 
 
@@ -83,10 +87,9 @@
             copies[-1].start()
     mine = group_ref[0]
     first.wait()
-    labels = label_ref[...]
     targets = []
     for side in range(2):
-        index = folded(labels, side * half, half)
+        index = folded(label_ref, side * half, half)
         rank, _, _ = ranked(index, regimes)
         place = jnp.where(mine == side, part - 1.0 - rank, rank - part)
         targets.append(jnp.where(place >= 0, index.astype(f32) * part + place, -1.0))
@@ -97,7 +100,7 @@
     for side in range(2):
         for m in range(rows):
             for t in range(pieces):
-                at = (m + rows * t, slice(side * half, (side + 1) * half))
+                at = (m * pieces + t, slice(side * half, (side + 1) * half))
                 columns.append(jnp.concatenate([heat_ref[at], moist_ref[at]], axis=1))
     soundings = jnp.concatenate(columns, axis=0)
     total = out_ref.shape[0]
@@ -116,12 +119,11 @@
 
 
 def plan_kernel(regimes, part, group_ref, label_ref, _, column_ref, pack_ref, crowd_ref):
-    labels = label_ref[...]
-    half = labels.shape[1] // 2
+    half = label_ref.shape[1] // 2
     mine = group_ref[0]
     sides = []
     for side in range(2):
-        index = folded(labels, side * half, half)
+        index = folded(label_ref, side * half, half)
         rank, member, count = ranked(index, regimes)
         sides.append((index.astype(f32), rank, member, jnp.maximum(count - part, 0.0)))
     index, rank, member, spare = [jnp.where(mine == 0, a, b) for a, b in zip(*sides)]
@@ -203,15 +205,25 @@
         ).astype(bf16)
 
 
-def place_kernel(column_ref, kept_ref, come_ref, heat_ref, moist_ref):
-    half, levels = heat_ref.shape[1:]
-    rows = heat_ref.shape[0] * half // LANES
+def place_kernel(column_ref, kept_ref, come_ref, heat_out, moist_out, heat_ref, moist_ref, sem):
+    deep, half, levels = heat_ref.shape
+    pieces = LANES // half
+    rows = deep // pieces
+    copies = []
     for m in range(rows):
         total = picked(column_ref[:, rows + m : rows + m + 1], come_ref)
         total = (total + kept_ref[m * LANES : (m + 1) * LANES].astype(f32)).astype(bf16)
-        for t in range(LANES // half):
-            heat_ref[m + rows * t] = total[t * half : (t + 1) * half, :levels]
-            moist_ref[m + rows * t] = total[t * half : (t + 1) * half, levels:]
+        for t in range(pieces):
+            heat_ref[m * pieces + t] = total[t * half : (t + 1) * half, :levels]
+            moist_ref[m * pieces + t] = total[t * half : (t + 1) * half, levels:]
+        if m % 2 == 1:
+            at = slice((m - 1) * pieces, (m + 1) * pieces)
+            for source, target in ((heat_ref, heat_out), (moist_ref, moist_out)):
+                copy = pltpu.make_async_copy(source.at[at], target.at[at], sem.at[len(copies)])
+                copy.start()
+                copies.append(copy)
+    for copy in copies:
+        copy.wait()
 
 
 def placed(room, shape, column_plan, pack_plan, result, after):
@@ -230,6 +242,9 @@
         pl.pallas_call(
             place_kernel,
             out_shape=(out, out),
+            out_specs=(HBM, HBM),
+            scratch_shapes=[pltpu.VMEM(shape, bf16)] * 2
+            + [pltpu.SemaphoreType.DMA((shape[0] * shape[1] // LANES,))],
             compiler_params=params(12),
             cost_estimate=cost(2 * shape[0] * shape[1] * come.size, 2 * MIB),
             name="place",

time: 60.3 us -> 60.3 us (level)
  no operation moved by 1% of the time
where the time goes in v4:
time: 60.3 us; the launch traced here: 59.8 us
  Pallas kernels  22.3 us (37%)
  starting transfers between devices  19.4 us (32%)
  waiting for transfers between devices  16.6 us (28%)
  between operations  1.42 us (2%)
    all_to_all x2, waiting for transfers between devices, swapped(): one = lax.all_to_all(one, 'blk', split_axis=0, concat_axis=0, tiled=True)  14.9 us
    all_to_all x2, starting transfers between devices, swapped(): one = lax.all_to_all(one, 'blk', split_axis=0, concat_axis=0, tiled=True)  13.3 us
    pallas_call x1, Pallas kernels, dynamics(): pl.pallas_call(dynamics_kernel, out_shape=(out,) * 3 + (TOKEN,), in_specs...  5.68 us
    ppermute x1, starting transfers between devices, halos(): lax.ppermute(head, 'blk', [((i + 1) % count, i) for i in range(count)])  4.04 us
    pallas_call x1, Pallas kernels, back(): pl.pallas_call(back_kernel, out_shape=(jax.ShapeDtypeStruct((rows, last.s...  3.92 us
    pallas_call x1, Pallas kernels, front(): pl.pallas_call(front_kernel, out_shape=jax.ShapeDtypeStruct((rows, hidden...  3.56 us
    pallas_call x1, Pallas kernels, local(): pl.pallas_call(functools.partial(route_kernel, regimes, part), out_shape=...  3.43 us
    ppermute x1, waiting for transfers between devices, placed(): come = lax.ppermute(packed, 'grp', [(0, 1), (1, 0)])  1.73 us
  transfers between devices with their start and end apart: 5, of which 3 were waited for; matrix products, arithmetic and copies ran while one was open for 0% of the time, Pallas kernels for 23%

profile of v4, /device:TPU:0, one launch (start us, length us, event | category | flops | bytes accessed | tf_op | source)
XLA Modules:
  0.0 59.8 jit_solution(2107383535546602873)
XLA Ops:
  0.6 3.4 %route.1 = (bf16[1024,256]{1,0:T(8,128)(2,1)}, f32[8,128]{1,0:T(8,128)S(1)}) custom-call(s32[1]{0:T(128)} %bitcast.group_ref, s32[32,64]{1,0:T(8,128)} %label_ref.1, bf16[32,64,128]{2,1,0:T(8,128)(2,1)} %heat_in.1, bf16[32,64,128]{2,1,0:T(8,128)(2,1)} %moist_in.1), custom_call_target="tpu_custom_call" | custom-call | flops 1073741824 | bytes 2097152 | tf_op jit(solution)/shard_map/route/pallas_call | solution.py:563
  4.1 7.4 %all-to-all-start = ((bf16[16,64,256]{2,1,0:T(8,128)(2,1)}), bf16[16,64,256]{2,1,0:T(8,128)(2,1)S(1)}, u32[]{:S(2)}, u32[]{:S(2)}) async-start(bf16[16,64,256]{2,1,0:T(8,128)(2,1)} %bitcast.2), calls=%async_computation | async-start | bytes 1048576 | tf_op jit(solution)/shard_map/all_to_all | solution.py:560
  11.5 1.3 %edges.1 = (bf16[21,40,128]{2,1,0:T(8,128)(2,1)S(1)}, bf16[21,40,128]{2,1,0:T(8,128)(2,1)S(1)}) custom-call(s32[1]{0:T(128)} %bitcast.group_ref, bf16[32,64,128]{2,1,0:T(8,128)(2,1)} %e_hbm.1, bf16[32,64,128]{2,1,0:T(8,128)(2,1)} %n_hbm.1, bf16[32,64,128]{2,1,0:T(8,128)(2,1)} %p_hbm.1, f32[8,128]{1,0:T(8,128)S(1)} %get-tuple-element.46._), custom_call_target="tpu_custom_call" | custom-call | flops 1048576 | bytes 2097152 | tf_op jit(solution)/shard_map/edges/pallas_call | solution.py:521
  12.8 0.5 collective-permute-start.2
  13.3 4.0 %collective-permute-start.3 = (bf16[21,40,128]{2,1,0:T(8,128)(2,1)S(1)}, bf16[21,40,128]{2,1,0:T(8,128)(2,1)S(1)}, u32[]{:S(2)}, u32[]{:S(2)}) collective-permute-start(bf16[21,40,128]{2,1,0:T(8,128)(2,1)S(1)} %get-tuple-element.48), channel_id=1, source_target_pairs={{1,0},{2,1},{3,2},{4,3},{5,4},{6,5},{7,6},{8,7},{9,8},{10,9},{11,1... | collective-permute-start | bytes 645128 | tf_op jit(solution)/shard_map/ppermute | solution.py:532
  17.3 1.4 %fetch.1 = (bf16[256,1024]{1,0:T(8,128)(2,1)S(1)}, bf16[1024,512]{1,0:T(8,128)(2,1)S(1)}) custom-call(bf16[1,256,1024]{2,1,0:T(8,128)(2,1)} %first_in.1, bf16[1,1024,1024]{2,1,0:T(8,128)(2,1)} %second_in.3, f32[8,128]{1,0:T(8,128)S(1)} %get-tuple-element.46._), custom_call_target="tpu_custom_call" | custom-call | bytes 1572864 | tf_op jit(solution)/shard_map/fetch/pallas_call | solution.py:283
  18.7 7.7 %all-to-all-done = bf16[16,64,256]{2,1,0:T(8,128)(2,1)S(1)} async-done(((bf16[16,64,256]{2,1,0:T(8,128)(2,1)}), bf16[16,64,256]{2,1,0:T(8,128)(2,1)S(1)}, u32[]{:S(2)}, u32[]{:S(2)}) %all-to-all-start) | async-done | bytes 524320 | tf_op jit(solution)/shard_map/all_to_all | solution.py:560
  26.4 0.0 copy-start.2
  26.4 0.0 copy-start.3
  26.4 3.6 %front.1.two_ref = bf16[1024,1024]{1,0:T(8,128)(2,1)S(1)} custom-call(bf16[1024,256]{1,0:T(8,128)(2,1)S(1)} %bitcast.9, bf16[256,1024]{1,0:T(8,128)(2,1)S(1)} %get-tuple-element.50.first_ref, bf16[1024,512]{1,0:T(8,128)(2,1)S(1)} %get-tuple-element.51.left_ref, bf16[1,1024,1024]{2,1,0:T(8,128)(2,1)} %second_in.3), custom_call_target="tpu_custom_call" | custom-call | flops 2684354560 | bytes 2621440 | tf_op jit(solution)/shard_map/front/pallas_call | solution.py:330
  30.0 0.0 collective-permute-done.2._.left_in
  30.0 0.0 collective-permute-done.3.__.right_in
  30.0 0.0 copy-done.2
  30.0 0.0 copy-done.3
  30.0 0.0 copy-start
  30.0 0.0 copy-start.1
  30.1 3.9 %back.1 = (bf16[1024,256]{1,0:T(8,128)(2,1)}, f32[8,128]{1,0:T(8,128)S(1)}) custom-call(bf16[1024,1024]{1,0:T(8,128)(2,1)S(1)} %front.1.two_ref, bf16[1024,1024]{1,0:T(8,128)(2,1)S(1)} %bitcast.11, bf16[1024,256]{1,0:T(8,128)(2,1)S(1)} %bitcast.12, bf16[21,40,128]{2,1,0:T(8,128)(2,1)S(1)} %collective-permute-done.2._.left_in, ...), custom_call_target="tpu_custom_call" | custom-call | flops 2684354560 | bytes 2621440 | tf_op jit(solution)/shard_map/back/pallas_call | solution.py:348
  34.0 5.9 %all-to-all-start.1 = ((bf16[16,64,256]{2,1,0:T(8,128)(2,1)}), bf16[16,64,256]{2,1,0:T(8,128)(2,1)S(1)}, u32[]{:S(2)}, u32[]{:S(2)}) async-start(bf16[16,64,256]{2,1,0:T(8,128)(2,1)} %bitcast.7), calls=%async_computation.1 | async-start | bytes 1048576 | tf_op jit(solution)/shard_map/all_to_all | solution.py:560
  39.9 0.0 copy-done
  39.9 0.9 %plan.1 = (f32[128,16]{1,0:T(8,128)S(1)}, f32[8,128]{1,0:T(8,128)S(1)}, s32[1]{0:T(128)}) custom-call(s32[1]{0:T(128)} %bitcast.group_ref, s32[32,64]{1,0:T(8,128)S(1)} %copy-done, f32[8,128]{1,0:T(8,128)S(1)} %get-tuple-element.46._), custom_call_target="tpu_custom_call" | custom-call | flops 1048576 | bytes 1048576 | tf_op jit(solution)/shard_map/plan/pallas_call | solution.py:156
  41.5 0.0 copy-done.1
  41.5 5.7 %dynamics.1 = (bf16[32,32,128]{2,1,0:T(8,128)(2,1)}, bf16[32,32,128]{2,1,0:T(8,128)(2,1)}, bf16[32,32,128]{2,1,0:T(8,128)(2,1)}, f32[8,128]{1,0:T(8,128)S(1)}) custom-call(s32[1]{0:T(128)} %bitcast.group_ref, f32[1,128]{1,0:T(1,128)S(1)} %bitcast.10, bf16[32,64,128]{2,1,0:T(8,128)(2,1)} %e_hbm.1, bf16[32,64,128]{2,1,0:T(8,128)(2,1)} %n_hbm.1, ...), custom_call_target="tpu_custom_call" | custom-call | flops 26214400 | bytes 3145728 | tf_op jit(solution)/shard_map/dynamics/pallas_call | solution.py:470
  47.2 7.2 %all-to-all-done.1 = bf16[16,64,256]{2,1,0:T(8,128)(2,1)S(1)} async-done(((bf16[16,64,256]{2,1,0:T(8,128)(2,1)}), bf16[16,64,256]{2,1,0:T(8,128)(2,1)S(1)}, u32[]{:S(2)}, u32[]{:S(2)}) %all-to-all-start.1) | async-done | bytes 524320 | tf_op jit(solution)/shard_map/all_to_all | solution.py:560
  54.4 5.4 %conditional.1 = ((bf16[32,32,128]{2,1,0:T(8,128)(2,1)}, bf16[32,32,128]{2,1,0:T(8,128)(2,1)})) conditional(s32[]{:T(128)} %bitcast.6, (f32[8,128]{1,0:T(8,128)S(1)}, bf16[1024,256]{1,0:T(8,128)(2,1)S(1)}, f32[8,128]{1,0:T(8,128)S(1)}, f32[128,16]{1,0:T(8,128)S(1)}) %tuple.20, (f32[8,128]{1,0:T(8,128)S(1)}, bf16[1024,256]{1,0:T(8,128)(2,1)S(1)}, ...), branch_computations={%region_0.0_spmd, %region_1.0_spmd} | conditional | flops 1073741824 | bytes 5242928 | solution.py:603
  54.4 0.2 pack.2.packed_ref
  54.6 1.6 %collective-permute-start = (bf16[80,256]{1,0:T(8,128)(2,1)S(1)}, bf16[80,256]{1,0:T(8,128)(2,1)S(1)}, u32[]{:S(2)}, u32[]{:S(2)}) collective-permute-start(bf16[80,256]{1,0:T(8,128)(2,1)S(1)} %pack.2.packed_ref), channel_id=1, source_target_pairs={{0,16},{16,0},{1,17},{17,1},{2,18},{18,2},{3,19},{19,3},{4,20},{20... | collective-permute-start | bytes 122888 | tf_op jit(solution)/shard_map/cond/branch_0_fun/ppermute | solution.py:231
  56.2 0.8 %keep.2.kept_ref = bf16[1024,256]{1,0:T(8,128)(2,1)S(1)} custom-call(f32[128,16]{1,0:T(8,128)S(1)} %get-tuple-element.16.column_ref, bf16[1024,256]{1,0:T(8,128)(2,1)S(1)} %get-tuple-element.17.result_ref, bf16[80,256]{1,0:T(8,128)(2,1)S(1)} %pack.2.packed_ref), custom_call_target="tpu_custom_call" | custom-call | flops 536870912 | bytes 1048576 | tf_op jit(solution)/shard_map/cond/branch_0_fun/keep/pallas_call | solution.py:232
  56.9 1.7 %collective-permute-done.come_ref = bf16[80,256]{1,0:T(8,128)(2,1)S(1)} collective-permute-done((bf16[80,256]{1,0:T(8,128)(2,1)S(1)}, bf16[80,256]{1,0:T(8,128)(2,1)S(1)}, u32[]{:S(2)}, u32[]{:S(2)}) %collective-permute-start) | collective-permute-done | bytes 40992 | tf_op jit(solution)/shard_map/cond/branch_0_fun/ppermute | solution.py:231
  58.7 1.1 %place.2 = (bf16[32,32,128]{2,1,0:T(8,128)(2,1)}, bf16[32,32,128]{2,1,0:T(8,128)(2,1)}) custom-call(f32[128,16]{1,0:T(8,128)S(1)} %get-tuple-element.16.column_ref, bf16[1024,256]{1,0:T(8,128)(2,1)S(1)} %keep.2.kept_ref, bf16[80,256]{1,0:T(8,128)(2,1)S(1)} %collective-permute-done.come_ref), custom_call_target="tpu_custom_call" | custom-call | flops 41943040 | bytes 2097152 | tf_op jit(solution)/shard_map/cond/branch_0_fun/place/pallas_call | solution.py:242
Async XLA Ops:
  4.1 22.3 %all-to-all-start = ((bf16[16,64,256]{2,1,0:T(8,128)(2,1)}), bf16[16,64,256]{2,1,0:T(8,128)(2,1)S(1)}, u32[]{:S(2)}, u32[]{:S(2)}) async-start(bf16[16,64,256]{2,1,0:T(8,128)(2,1)} %bitcast.2), calls=%async_computation | async-start | bytes 1048576 | tf_op jit(solution)/shard_map/all_to_all | solution.py:560
  12.8 17.2 %collective-permute-start.2 = (bf16[21,40,128]{2,1,0:T(8,128)(2,1)S(1)}, bf16[21,40,128]{2,1,0:T(8,128)(2,1)S(1)}, u32[]{:S(2)}, u32[]{:S(2)}) collective-permute-start(bf16[21,40,128]{2,1,0:T(8,128)(2,1)S(1)} %get-tuple-element.47), channel_id=1, source_target_pairs={{0,1},{1,2},{2,3},{3,4},{4,5},{5,6},{6,7},{7,8},{8,9},{9,10},{10,1... | collective-permute-start | bytes 645128 | tf_op jit(solution)/shard_map/ppermute | solution.py:531
  13.3 16.7 %collective-permute-start.3 = (bf16[21,40,128]{2,1,0:T(8,128)(2,1)S(1)}, bf16[21,40,128]{2,1,0:T(8,128)(2,1)S(1)}, u32[]{:S(2)}, u32[]{:S(2)}) collective-permute-start(bf16[21,40,128]{2,1,0:T(8,128)(2,1)S(1)} %get-tuple-element.48), channel_id=1, source_target_pairs={{1,0},{2,1},{3,2},{4,3},{5,4},{6,5},{7,6},{8,7},{9,8},{10,9},{11,1... | collective-permute-start | bytes 645128 | tf_op jit(solution)/shard_map/ppermute | solution.py:532
  26.4 3.6 %copy-start.2 = (bf16[1,1024,1024]{2,1,0:T(8,128)(2,1)S(1)}, bf16[1,1024,1024]{2,1,0:T(8,128)(2,1)}, u32[]{:S(2)}) copy-start(bf16[1,1024,1024]{2,1,0:T(8,128)(2,1)} %param.22) | copy-start | bytes 6291460
  26.4 3.6 %copy-start.3 = (bf16[1,1024,256]{2,1,0:T(8,128)(2,1)S(1)}, bf16[1,1024,256]{2,1,0:T(8,128)(2,1)}, u32[]{:S(2)}) copy-start(bf16[1,1024,256]{2,1,0:T(8,128)(2,1)} %param.23) | copy-start | bytes 1572868
  30.0 9.9 %copy-start = (s32[32,64]{1,0:T(8,128)S(1)}, s32[32,64]{1,0:T(8,128)}, u32[]{:S(2)}) copy-start(s32[32,64]{1,0:T(8,128)} %label_ref.1) | copy-start | bytes 24580
  30.0 11.5 %copy-start.1 = (f32[128]{0:T(128)S(1)}, f32[128]{0:T(128)}, u32[]{:S(2)}) copy-start(f32[128]{0:T(128)} %param.19) | copy-start | bytes 1540
  34.0 20.4 %all-to-all-start.1 = ((bf16[16,64,256]{2,1,0:T(8,128)(2,1)}), bf16[16,64,256]{2,1,0:T(8,128)(2,1)S(1)}, u32[]{:S(2)}, u32[]{:S(2)}) async-start(bf16[16,64,256]{2,1,0:T(8,128)(2,1)} %bitcast.7), calls=%async_computation.1 | async-start | bytes 1048576 | tf_op jit(solution)/shard_map/all_to_all | solution.py:560
  54.6 4.1 %collective-permute-start = (bf16[80,256]{1,0:T(8,128)(2,1)S(1)}, bf16[80,256]{1,0:T(8,128)(2,1)S(1)}, u32[]{:S(2)}, u32[]{:S(2)}) collective-permute-start(bf16[80,256]{1,0:T(8,128)(2,1)S(1)} %pack.2.packed_ref), channel_id=1, source_target_pairs={{0,16},{16,0},{1,17},{17,1},{2,18},{18,2},{3,19},{19,3},{4,20},{20... | collective-permute-start | bytes 122888 | tf_op jit(solution)/shard_map/cond/branch_0_fun/ppermute | solution.py:231

commit v5 on v4

--- a/solution.py
+++ b/solution.py
@@ -69,7 +69,7 @@
 
 
 def route_kernel(
-    regimes, part, group_ref, label_in, heat_in, moist_in, out_ref, token_ref, label_ref, heat_ref, moist_ref, sem
+    regimes, part, label_in, heat_in, moist_in, out_hbm, token_ref, label_ref, heat_ref, moist_ref, out_ref, sem, out_sem
 ):
     token_ref[...] = jnp.zeros_like(token_ref)
     deep, wide, levels = heat_ref.shape
@@ -85,7 +85,7 @@
             n = len(copies) + 1
             copies.append(pltpu.make_async_copy(source.at[at], target.at[at], sem.at[n]))
             copies[-1].start()
-    mine = group_ref[0]
+    mine = lax.axis_index("grp")
     first.wait()
     targets = []
     for side in range(2):
@@ -107,6 +107,7 @@
     tile = min(256, total)
     slot = lax.broadcasted_iota(i32, (tile, LANES), 0).astype(f32).astype(bf16)
     yes, no = jnp.ones((), bf16), jnp.zeros((), bf16)
+    sends = []
     for start in range(0, total, tile):
         near = target - start
         near = jnp.where((near >= 0) & (near < tile), near, -1.0).astype(bf16)
@@ -116,11 +117,16 @@
         out_ref[start : start + tile] = jnp.dot(
             picks, soundings, preferred_element_type=f32
         ).astype(bf16)
-
-
-def plan_kernel(regimes, part, group_ref, label_ref, _, column_ref, pack_ref, crowd_ref):
+        at = slice(start, start + tile)
+        sends.append(pltpu.make_async_copy(out_ref.at[at], out_hbm.at[at], out_sem.at[start // tile]))
+        sends[-1].start()
+    for send in sends:
+        send.wait()
+
+
+def plan_kernel(regimes, part, label_ref, _, column_ref, pack_ref, crowd_ref):
     half = label_ref.shape[1] // 2
-    mine = group_ref[0]
+    mine = lax.axis_index("grp")
     sides = []
     for side in range(2):
         index = folded(label_ref, side * half, half)
@@ -152,7 +158,7 @@
             pack_ref[r // per_row : r // per_row + 1] = line
 
 
-def plan(regimes, part, rows, group, labels, after):
+def plan(regimes, part, rows, labels, after):
     return pl.pallas_call(
         functools.partial(plan_kernel, regimes, part),
         out_shape=(
@@ -160,12 +166,12 @@
             jax.ShapeDtypeStruct((regimes * part // LANES, LANES), f32),
             jax.ShapeDtypeStruct((1,), i32),
         ),
-        in_specs=[SMEM, VMEM, VMEM],
+        in_specs=[VMEM, VMEM],
         out_specs=(VMEM, VMEM, SMEM),
         compiler_params=params(12),
         cost_estimate=cost(MIB, MIB),
         name="plan",
-    )(group, labels, after)
+    )(labels, after)
 
 
 def pack_kernel(pack_ref, result_ref, _, out_ref):
@@ -362,7 +368,7 @@
 
 
 def dynamics_kernel(
-    group_ref, rate_ref, e_hbm, n_hbm, p_hbm, left_in, right_in, _, e_out, n_out, p_out, token_ref,
+    rate_ref, e_hbm, n_hbm, p_hbm, left_in, right_in, _, e_out, n_out, p_out, token_ref,
     e_ref, n_ref, p_ref, e_in, n_in, p_in, left_ref, right_ref, sem,
 ):
     inputs = [
@@ -382,7 +388,7 @@
     span = e_ref.shape[1]
     reach = span - half
     wide = e_in.shape[1]
-    mine = group_ref[0]
+    mine = lax.axis_index("grp")
     coef = rate_ref[...] * 0.5
 
     edge = jnp.zeros((8, LANES), f32)
@@ -460,7 +466,7 @@
     lax.fori_loop(0, deep, store, 0)
 
 
-def dynamics(group, rate, e, n, p, left, right, after):
+def dynamics(rate, e, n, p, left, right, after):
     deep, wide, levels = e.shape
     half = wide // 2
     reach = 2 * SUB
@@ -470,7 +476,7 @@
     return pl.pallas_call(
         dynamics_kernel,
         out_shape=(out,) * 3 + (TOKEN,),
-        in_specs=[SMEM, VMEM] + [HBM] * 3 + [ANY] * 2 + [VMEM],
+        in_specs=[VMEM] + [HBM] * 3 + [ANY] * 2 + [VMEM],
         scratch_shapes=[
             pltpu.VMEM((deep + 2 * (reach - 1), span, levels), f32),
             pltpu.VMEM((deep + 2 * (reach - 2), span + 16, levels), f32),
@@ -483,13 +489,13 @@
         compiler_params=params(12),
         cost_estimate=cost(cells * 200, cells * 24),
         name="dynamics",
-    )(group, rate, *in_hbm(e, n, p), left, right, after)
-
-
-def edges_kernel(group_ref, e_in, n_in, p_in, _, tail_ref, head_ref, last_ref, first_ref, sem):
+    )(rate, *in_hbm(e, n, p), left, right, after)
+
+
+def edges_kernel(e_in, n_in, p_in, _, tail_ref, head_ref, last_ref, first_ref, sem):
     deep, wide = e_in.shape[:2]
     span = tail_ref.shape[1]
-    mine = group_ref[0]
+    mine = lax.axis_index("grp")
     reach = 2 * SUB
     copies = []
     at = 0
@@ -513,7 +519,7 @@
             out[i] = jnp.where(mine == 0, whole[:span], whole[wide - span :]).astype(bf16)
 
 
-def halos(group, e, n, p, after):
+def halos(e, n, p, after):
     wide, levels = e.shape[1:]
     reach = 2 * SUB
     count = lax.axis_size("blk")
@@ -521,13 +527,13 @@
     tail, head = pl.pallas_call(
         edges_kernel,
         out_shape=(out, out),
-        in_specs=[SMEM] + [HBM] * 3 + [VMEM],
+        in_specs=[HBM] * 3 + [VMEM],
         scratch_shapes=[pltpu.VMEM((3 * reach - 3, wide, levels), bf16)] * 2
         + [pltpu.SemaphoreType.DMA((6,))],
         compiler_params=params(6),
         cost_estimate=cost(MIB, 2 * MIB),
         name="edges",
-    )(group, *in_hbm(e, n, p), after)
+    )(*in_hbm(e, n, p), after)
     left = lax.ppermute(tail, "blk", [(i, (i + 1) % count) for i in range(count)])
     right = lax.ppermute(head, "blk", [((i + 1) % count, i) for i in range(count)])
     return left, right
@@ -546,7 +552,6 @@
     closing_dense_matrix,
     final_readout_matrix,
 ):
-    group = jnp.full((1,), lax.axis_index("grp"), i32)
     regimes = lax.axis_size("blk")
     deep, wide, levels = zonal_velocity_field.shape
     half = wide // 2
@@ -563,25 +568,27 @@
     sent, routed = pl.pallas_call(
         functools.partial(route_kernel, regimes, part),
         out_shape=(jax.ShapeDtypeStruct((size, profile), bf16), TOKEN),
-        in_specs=[SMEM, HBM, HBM, HBM],
+        in_specs=[HBM, HBM, HBM],
+        out_specs=(HBM, VMEM),
         scratch_shapes=[
             pltpu.VMEM((deep, wide), i32),
             pltpu.VMEM((deep, wide, levels), bf16),
             pltpu.VMEM((deep, wide, levels), bf16),
+            pltpu.VMEM((size, profile), bf16),
             pltpu.SemaphoreType.DMA((1 + 2 * (LANES // half),)),
+            pltpu.SemaphoreType.DMA((-(-size // 256),)),
         ],
         compiler_params=params(16),
         cost_estimate=cost(2 * size * deep * wide * profile, 2 * MIB),
         name="route",
     )(
-        group,
         *in_hbm(flow_category_label, delayed_thermal_deviation, delayed_moisture_deviation),
     )
     arrived = swapped(sent)
     left, right = halos(
-        group, zonal_velocity_field, meridional_velocity_field, barometric_disturbance, routed
-    )
-    column_plan, pack_plan, crowded = plan(regimes, part, rows, group, flow_category_label, routed)
+        zonal_velocity_field, meridional_velocity_field, barometric_disturbance, routed
+    )
+    column_plan, pack_plan, crowded = plan(regimes, part, rows, flow_category_label, routed)
     two = front(
         arrived,
         *fetched(initial_dense_matrix, middle_dense_matrix, routed),
@@ -590,7 +597,6 @@
     result, worked = back(two, closing_dense_matrix[0], final_readout_matrix[0], left, right)
     returned = swapped(result)
     east, north, pressure, moved = dynamics(
-        group,
         advective_stability_number.reshape(1, levels),
         zonal_velocity_field,
         meridional_velocity_field,

time: 60.3 us -> 60.2 us (level)
  no operation moved by 1% of the time
where the time goes in v5:
time: 60.2 us; the launch traced here: 59.7 us
  Pallas kernels  22.3 us (37%)
  starting transfers between devices  19.4 us (32%)
  waiting for transfers between devices  16.6 us (28%)
  between operations  1.42 us (2%)
    all_to_all x2, waiting for transfers between devices, swapped(): one = lax.all_to_all(one, 'blk', split_axis=0, concat_axis=0, tiled=True)  14.9 us
    all_to_all x2, starting transfers between devices, swapped(): one = lax.all_to_all(one, 'blk', split_axis=0, concat_axis=0, tiled=True)  13.3 us
    pallas_call x1, Pallas kernels, dynamics(): pl.pallas_call(dynamics_kernel, out_shape=(out,) * 3 + (TOKEN,), in_specs...  5.68 us
    ppermute x1, starting transfers between devices, halos(): lax.ppermute(head, 'blk', [((i + 1) % count, i) for i in range(count)])  4.04 us
    pallas_call x1, Pallas kernels, back(): pl.pallas_call(back_kernel, out_shape=(jax.ShapeDtypeStruct((rows, last.s...  3.92 us
    pallas_call x1, Pallas kernels, front(): pl.pallas_call(front_kernel, out_shape=jax.ShapeDtypeStruct((rows, hidden...  3.57 us
    pallas_call x1, Pallas kernels, local(): pl.pallas_call(functools.partial(route_kernel, regimes, part), out_shape=...  3.35 us
    ppermute x1, waiting for transfers between devices, placed(): come = lax.ppermute(packed, 'grp', [(0, 1), (1, 0)])  1.74 us
  transfers between devices with their start and end apart: 5, of which 3 were waited for; matrix products, arithmetic and copies ran while one was open for 0% of the time, Pallas kernels for 23%

profile of v5, /device:TPU:0, one launch (start us, length us, event | category | flops | bytes accessed | tf_op | source)
XLA Modules:
  0.0 59.7 jit_solution(13880700374240939772)
XLA Ops:
  0.6 3.3 %route.1 = (bf16[1024,256]{1,0:T(8,128)(2,1)}, f32[8,128]{1,0:T(8,128)S(1)}) custom-call(s32[32,64]{1,0:T(8,128)} %label_ref.1, bf16[32,64,128]{2,1,0:T(8,128)(2,1)} %heat_in.1, bf16[32,64,128]{2,1,0:T(8,128)(2,1)} %moist_in.1), custom_call_target="tpu_custom_call" | custom-call | flops 1073741824 | bytes 2097152 | tf_op jit(solution)/shard_map/route/pallas_call | solution.py:568
  4.0 7.4 %all-to-all-start = ((bf16[16,64,256]{2,1,0:T(8,128)(2,1)}), bf16[16,64,256]{2,1,0:T(8,128)(2,1)S(1)}, u32[]{:S(2)}, u32[]{:S(2)}) async-start(bf16[16,64,256]{2,1,0:T(8,128)(2,1)} %bitcast.1), calls=%async_computation | async-start | bytes 1048576 | tf_op jit(solution)/shard_map/all_to_all | solution.py:565
  11.4 1.3 %edges.1 = (bf16[21,40,128]{2,1,0:T(8,128)(2,1)S(1)}, bf16[21,40,128]{2,1,0:T(8,128)(2,1)S(1)}) custom-call(bf16[32,64,128]{2,1,0:T(8,128)(2,1)} %e_hbm.1, bf16[32,64,128]{2,1,0:T(8,128)(2,1)} %n_hbm.1, bf16[32,64,128]{2,1,0:T(8,128)(2,1)} %p_hbm.1, f32[8,128]{1,0:T(8,128)S(1)} %get-tuple-element.46._), custom_call_target="tpu_custom_call" | custom-call | flops 1048576 | bytes 2097152 | tf_op jit(solution)/shard_map/edges/pallas_call | solution.py:527
  12.7 0.5 collective-permute-start.2
  13.2 4.0 %collective-permute-start.3 = (bf16[21,40,128]{2,1,0:T(8,128)(2,1)S(1)}, bf16[21,40,128]{2,1,0:T(8,128)(2,1)S(1)}, u32[]{:S(2)}, u32[]{:S(2)}) collective-permute-start(bf16[21,40,128]{2,1,0:T(8,128)(2,1)S(1)} %get-tuple-element.48), channel_id=1, source_target_pairs={{1,0},{2,1},{3,2},{4,3},{5,4},{6,5},{7,6},{8,7},{9,8},{10,9},{11,1... | collective-permute-start | bytes 645128 | tf_op jit(solution)/shard_map/ppermute | solution.py:538
  17.2 1.4 %fetch.1 = (bf16[256,1024]{1,0:T(8,128)(2,1)S(1)}, bf16[1024,512]{1,0:T(8,128)(2,1)S(1)}) custom-call(bf16[1,256,1024]{2,1,0:T(8,128)(2,1)} %first_in.1, bf16[1,1024,1024]{2,1,0:T(8,128)(2,1)} %second_in.3, f32[8,128]{1,0:T(8,128)S(1)} %get-tuple-element.46._), custom_call_target="tpu_custom_call" | custom-call | bytes 1572864 | tf_op jit(solution)/shard_map/fetch/pallas_call | solution.py:289
  18.6 7.7 %all-to-all-done = bf16[16,64,256]{2,1,0:T(8,128)(2,1)S(1)} async-done(((bf16[16,64,256]{2,1,0:T(8,128)(2,1)}), bf16[16,64,256]{2,1,0:T(8,128)(2,1)S(1)}, u32[]{:S(2)}, u32[]{:S(2)}) %all-to-all-start) | async-done | bytes 524320 | tf_op jit(solution)/shard_map/all_to_all | solution.py:565
  26.3 0.0 copy-start.2
  26.3 0.0 copy-start.3
  26.3 3.6 %front.1.two_ref = bf16[1024,1024]{1,0:T(8,128)(2,1)S(1)} custom-call(bf16[1024,256]{1,0:T(8,128)(2,1)S(1)} %bitcast.8, bf16[256,1024]{1,0:T(8,128)(2,1)S(1)} %get-tuple-element.50.first_ref, bf16[1024,512]{1,0:T(8,128)(2,1)S(1)} %get-tuple-element.51.left_ref, bf16[1,1024,1024]{2,1,0:T(8,128)(2,1)} %second_in.3), custom_call_target="tpu_custom_call" | custom-call | flops 2684354560 | bytes 2621440 | tf_op jit(solution)/shard_map/front/pallas_call | solution.py:336
  29.9 0.0 collective-permute-done.2._.left_in
  29.9 0.0 collective-permute-done.3.__.right_in
  29.9 0.0 copy-done.2
  30.0 0.0 copy-done.3
  30.0 0.0 copy-start
  30.0 0.0 copy-start.1
  30.0 3.9 %back.1 = (bf16[1024,256]{1,0:T(8,128)(2,1)}, f32[8,128]{1,0:T(8,128)S(1)}) custom-call(bf16[1024,1024]{1,0:T(8,128)(2,1)S(1)} %front.1.two_ref, bf16[1024,1024]{1,0:T(8,128)(2,1)S(1)} %bitcast.10, bf16[1024,256]{1,0:T(8,128)(2,1)S(1)} %bitcast.11, bf16[21,40,128]{2,1,0:T(8,128)(2,1)S(1)} %collective-permute-done.2._.left_in, ...), custom_call_target="tpu_custom_call" | custom-call | flops 2684354560 | bytes 2621440 | tf_op jit(solution)/shard_map/back/pallas_call | solution.py:354
  33.9 5.9 %all-to-all-start.1 = ((bf16[16,64,256]{2,1,0:T(8,128)(2,1)}), bf16[16,64,256]{2,1,0:T(8,128)(2,1)S(1)}, u32[]{:S(2)}, u32[]{:S(2)}) async-start(bf16[16,64,256]{2,1,0:T(8,128)(2,1)} %bitcast.6), calls=%async_computation.1 | async-start | bytes 1048576 | tf_op jit(solution)/shard_map/all_to_all | solution.py:565
  39.9 0.0 copy-done
  39.9 0.9 %plan.1 = (f32[128,16]{1,0:T(8,128)S(1)}, f32[8,128]{1,0:T(8,128)S(1)}, s32[1]{0:T(128)}) custom-call(s32[32,64]{1,0:T(8,128)S(1)} %copy-done, f32[8,128]{1,0:T(8,128)S(1)} %get-tuple-element.46._), custom_call_target="tpu_custom_call" | custom-call | flops 1048576 | bytes 1048576 | tf_op jit(solution)/shard_map/plan/pallas_call | solution.py:162
  41.4 0.0 copy-done.1
  41.5 5.7 %dynamics.1 = (bf16[32,32,128]{2,1,0:T(8,128)(2,1)}, bf16[32,32,128]{2,1,0:T(8,128)(2,1)}, bf16[32,32,128]{2,1,0:T(8,128)(2,1)}, f32[8,128]{1,0:T(8,128)S(1)}) custom-call(f32[1,128]{1,0:T(1,128)S(1)} %bitcast.9, bf16[32,64,128]{2,1,0:T(8,128)(2,1)} %e_hbm.1, bf16[32,64,128]{2,1,0:T(8,128)(2,1)} %n_hbm.1, bf16[32,64,128]{2,1,0:T(8,128)(2,1)} %p_hbm.1, ...), custom_call_target="tpu_custom_call" | custom-call | flops 26214400 | bytes 3145728 | tf_op jit(solution)/shard_map/dynamics/pallas_call | solution.py:476
  47.1 7.2 %all-to-all-done.1 = bf16[16,64,256]{2,1,0:T(8,128)(2,1)S(1)} async-done(((bf16[16,64,256]{2,1,0:T(8,128)(2,1)}), bf16[16,64,256]{2,1,0:T(8,128)(2,1)S(1)}, u32[]{:S(2)}, u32[]{:S(2)}) %all-to-all-start.1) | async-done | bytes 524320 | tf_op jit(solution)/shard_map/all_to_all | solution.py:565
  54.3 5.4 %conditional.1 = ((bf16[32,32,128]{2,1,0:T(8,128)(2,1)}, bf16[32,32,128]{2,1,0:T(8,128)(2,1)})) conditional(s32[]{:T(128)} %bitcast.5, (f32[8,128]{1,0:T(8,128)S(1)}, bf16[1024,256]{1,0:T(8,128)(2,1)S(1)}, f32[8,128]{1,0:T(8,128)S(1)}, f32[128,16]{1,0:T(8,128)S(1)}) %tuple.20, (f32[8,128]{1,0:T(8,128)S(1)}, bf16[1024,256]{1,0:T(8,128)(2,1)S(1)}, ...), branch_computations={%region_0.0_spmd, %region_1.0_spmd} | conditional | flops 1073741824 | bytes 5242928 | solution.py:609
  54.3 0.2 pack.2.packed_ref
  54.5 1.6 %collective-permute-start = (bf16[80,256]{1,0:T(8,128)(2,1)S(1)}, bf16[80,256]{1,0:T(8,128)(2,1)S(1)}, u32[]{:S(2)}, u32[]{:S(2)}) collective-permute-start(bf16[80,256]{1,0:T(8,128)(2,1)S(1)} %pack.2.packed_ref), channel_id=1, source_target_pairs={{0,16},{16,0},{1,17},{17,1},{2,18},{18,2},{3,19},{19,3},{4,20},{20... | collective-permute-start | bytes 122888 | tf_op jit(solution)/shard_map/cond/branch_0_fun/ppermute | solution.py:237
  56.1 0.8 %keep.2.kept_ref = bf16[1024,256]{1,0:T(8,128)(2,1)S(1)} custom-call(f32[128,16]{1,0:T(8,128)S(1)} %get-tuple-element.16.column_ref, bf16[1024,256]{1,0:T(8,128)(2,1)S(1)} %get-tuple-element.17.result_ref, bf16[80,256]{1,0:T(8,128)(2,1)S(1)} %pack.2.packed_ref), custom_call_target="tpu_custom_call" | custom-call | flops 536870912 | bytes 1048576 | tf_op jit(solution)/shard_map/cond/branch_0_fun/keep/pallas_call | solution.py:238
  56.9 1.7 %collective-permute-done.come_ref = bf16[80,256]{1,0:T(8,128)(2,1)S(1)} collective-permute-done((bf16[80,256]{1,0:T(8,128)(2,1)S(1)}, bf16[80,256]{1,0:T(8,128)(2,1)S(1)}, u32[]{:S(2)}, u32[]{:S(2)}) %collective-permute-start) | collective-permute-done | bytes 40992 | tf_op jit(solution)/shard_map/cond/branch_0_fun/ppermute | solution.py:237
  58.6 1.1 %place.2 = (bf16[32,32,128]{2,1,0:T(8,128)(2,1)}, bf16[32,32,128]{2,1,0:T(8,128)(2,1)}) custom-call(f32[128,16]{1,0:T(8,128)S(1)} %get-tuple-element.16.column_ref, bf16[1024,256]{1,0:T(8,128)(2,1)S(1)} %keep.2.kept_ref, bf16[80,256]{1,0:T(8,128)(2,1)S(1)} %collective-permute-done.come_ref), custom_call_target="tpu_custom_call" | custom-call | flops 41943040 | bytes 2097152 | tf_op jit(solution)/shard_map/cond/branch_0_fun/place/pallas_call | solution.py:248
Async XLA Ops:
  4.0 22.3 %all-to-all-start = ((bf16[16,64,256]{2,1,0:T(8,128)(2,1)}), bf16[16,64,256]{2,1,0:T(8,128)(2,1)S(1)}, u32[]{:S(2)}, u32[]{:S(2)}) async-start(bf16[16,64,256]{2,1,0:T(8,128)(2,1)} %bitcast.1), calls=%async_computation | async-start | bytes 1048576 | tf_op jit(solution)/shard_map/all_to_all | solution.py:565
  12.7 17.2 %collective-permute-start.2 = (bf16[21,40,128]{2,1,0:T(8,128)(2,1)S(1)}, bf16[21,40,128]{2,1,0:T(8,128)(2,1)S(1)}, u32[]{:S(2)}, u32[]{:S(2)}) collective-permute-start(bf16[21,40,128]{2,1,0:T(8,128)(2,1)S(1)} %get-tuple-element.47), channel_id=1, source_target_pairs={{0,1},{1,2},{2,3},{3,4},{4,5},{5,6},{6,7},{7,8},{8,9},{9,10},{10,1... | collective-permute-start | bytes 645128 | tf_op jit(solution)/shard_map/ppermute | solution.py:537
  13.2 16.7 %collective-permute-start.3 = (bf16[21,40,128]{2,1,0:T(8,128)(2,1)S(1)}, bf16[21,40,128]{2,1,0:T(8,128)(2,1)S(1)}, u32[]{:S(2)}, u32[]{:S(2)}) collective-permute-start(bf16[21,40,128]{2,1,0:T(8,128)(2,1)S(1)} %get-tuple-element.48), channel_id=1, source_target_pairs={{1,0},{2,1},{3,2},{4,3},{5,4},{6,5},{7,6},{8,7},{9,8},{10,9},{11,1... | collective-permute-start | bytes 645128 | tf_op jit(solution)/shard_map/ppermute | solution.py:538
  26.3 3.6 %copy-start.2 = (bf16[1,1024,1024]{2,1,0:T(8,128)(2,1)S(1)}, bf16[1,1024,1024]{2,1,0:T(8,128)(2,1)}, u32[]{:S(2)}) copy-start(bf16[1,1024,1024]{2,1,0:T(8,128)(2,1)} %param.22) | copy-start | bytes 6291460
  26.3 3.6 %copy-start.3 = (bf16[1,1024,256]{2,1,0:T(8,128)(2,1)S(1)}, bf16[1,1024,256]{2,1,0:T(8,128)(2,1)}, u32[]{:S(2)}) copy-start(bf16[1,1024,256]{2,1,0:T(8,128)(2,1)} %param.23) | copy-start | bytes 1572868
  30.0 9.9 %copy-start = (s32[32,64]{1,0:T(8,128)S(1)}, s32[32,64]{1,0:T(8,128)}, u32[]{:S(2)}) copy-start(s32[32,64]{1,0:T(8,128)} %label_ref.1) | copy-start | bytes 24580
  30.0 11.5 %copy-start.1 = (f32[128]{0:T(128)S(1)}, f32[128]{0:T(128)}, u32[]{:S(2)}) copy-start(f32[128]{0:T(128)} %param.19) | copy-start | bytes 1540
  33.9 20.4 %all-to-all-start.1 = ((bf16[16,64,256]{2,1,0:T(8,128)(2,1)}), bf16[16,64,256]{2,1,0:T(8,128)(2,1)S(1)}, u32[]{:S(2)}, u32[]{:S(2)}) async-start(bf16[16,64,256]{2,1,0:T(8,128)(2,1)} %bitcast.6), calls=%async_computation.1 | async-start | bytes 1048576 | tf_op jit(solution)/shard_map/all_to_all | solution.py:565
  54.5 4.1 %collective-permute-start = (bf16[80,256]{1,0:T(8,128)(2,1)S(1)}, bf16[80,256]{1,0:T(8,128)(2,1)S(1)}, u32[]{:S(2)}, u32[]{:S(2)}) collective-permute-start(bf16[80,256]{1,0:T(8,128)(2,1)S(1)} %pack.2.packed_ref), channel_id=1, source_target_pairs={{0,16},{16,0},{1,17},{17,1},{2,18},{18,2},{3,19},{19,3},{4,20},{20... | collective-permute-start | bytes 122888 | tf_op jit(solution)/shard_map/cond/branch_0_fun/ppermute | solution.py:237
